TPU v7x, 32 devices: a whole 2x2x4 slice. The times are simulated.
32 devices in a mesh: seq: 8 (over y, x, core), tp: 4 (over z).
Axes of the slice: x: 2, y: 2, z: 4, core: 2. Of those that a mesh axis runs over, the one named last changes fastest.
Arguments:
- queries: bfloat16 [2048, 4096], P('seq', 'tp'), may hold values from -5 to 5
- keys: bfloat16 [2048, 1024], P('seq'), may hold values from -5 to 5
- values: bfloat16 [2048, 1024], P('seq'), may hold values from -6 to 6
- out_weight: bfloat16 [4096, 5120], P('tp'), may hold values from -0.29882812 to 0.29882812
Outputs:
- projected: bfloat16 [2048, 5120], P(('seq', 'tp'))
All inputs are finite; a program needn't handle non-finite values.
Results may differ from a plain program's by a relative error of at most 0.012.
Values may be sent and summed in bfloat16 or wider, within the bound.
No kernel may reach another device: no remote copies, remote signals or barrier semaphores. Data moves between devices by JAX's collectives and lax.ppermute only.
A program may use at most 64 MiB of HBM per device.

v0:
```python
import jax
import jax.numpy as jnp
from jax import lax
from jax.sharding import PartitionSpec as P

QUERY_HEADS = 32
KEY_VALUE_HEADS = 8
HEAD_DIMENSION = 128
STRETCH = 8192


def passed_along(block, axis, distance):
    devices = range(lax.axis_size(axis))
    route = [(i - distance, i) for i in devices if i - distance in devices]
    return lax.ppermute(block, axis, route)


def body(queries, keys, values, out_weight):
    tok = queries.shape[0]
    heads_here = queries.shape[1] // HEAD_DIMENSION
    query_group = QUERY_HEADS // KEY_VALUE_HEADS
    kv_here = max(1, heads_here // query_group)
    per_kv = heads_here // kv_here
    scale = HEAD_DIMENSION ** (-0.5)
    tp_place = lax.axis_index("tp")
    kv_first = tp_place * heads_here // query_group
    k_own = lax.dynamic_slice_in_dim(keys, kv_first * HEAD_DIMENSION, kv_here * HEAD_DIMENSION, 1)
    v_own = lax.dynamic_slice_in_dim(values, kv_first * HEAD_DIMENSION, kv_here * HEAD_DIMENSION, 1)
    seq_devs = lax.axis_size("seq")
    stretch_devs = min(STRETCH // tok, seq_devs)
    stretch_amount = tok * stretch_devs
    my_start = lax.axis_index("seq") * tok
    q_pos = my_start + jnp.arange(tok)
    q_split = queries.reshape(tok, kv_here, per_kv, HEAD_DIMENSION)

    def fold_block(state, pair, key_start):
        k_rows = pair[0].reshape(tok, kv_here, HEAD_DIMENSION)
        v_rows = pair[1].reshape(tok, kv_here, HEAD_DIMENSION)
        score = (
            jnp.einsum("tgrd,sgd->tgrs", q_split, k_rows, preferred_element_type=jnp.float32)
            * scale
        )
        k_pos = key_start + jnp.arange(tok)
        valid = (k_pos[None, :] <= q_pos[:, None]) & (
            k_pos[None, :] // stretch_amount == q_pos[:, None] // stretch_amount
        )
        score = jnp.where(valid[:, None, None, :], score, -1e30)
        top_old, total, accum = state
        top_new = jnp.maximum(top_old, jnp.max(score, axis=3))
        shrink = jnp.exp(top_old - top_new)
        weight = jnp.exp(score - top_new[..., None])
        total = total * shrink + jnp.sum(weight, axis=3)
        mixed = jnp.einsum(
            "tgrs,sgd->tgrd",
            weight.astype(jnp.bfloat16),
            v_rows,
            preferred_element_type=jnp.float32,
        )
        accum = accum * shrink[..., None] + mixed
        return (top_new, total, accum)

    start_state = (
        jnp.full((tok, kv_here, per_kv), -1e30, jnp.float32),
        jnp.zeros((tok, kv_here, per_kv), jnp.float32),
        jnp.zeros((tok, kv_here, per_kv, HEAD_DIMENSION), jnp.float32),
    )
    own_pair = jnp.stack([k_own, v_own])
    state = fold_block(start_state, own_pair, my_start)
    buffer = own_pair[None]
    reach = 1
    while reach < stretch_devs:
        incoming = passed_along(buffer, "seq", reach)

        def take(index, inner, incoming=incoming, reach=reach):
            pair = lax.dynamic_index_in_dim(incoming, index, 0, keepdims=False)
            return fold_block(inner, pair, my_start - (reach + index) * tok)

        state = lax.fori_loop(0, reach, take, state)
        buffer = jnp.concatenate([buffer, incoming], axis=0)
        reach = reach * 2
    top_val, total, accum = state
    attended = (
        (accum / total[..., None]).astype(jnp.bfloat16).reshape(tok, heads_here * HEAD_DIMENSION)
    )
    return lax.psum_scatter(
        jnp.dot(attended, out_weight, preferred_element_type=jnp.float32).astype(jnp.bfloat16),
        "tp",
        scatter_dimension=0,
        tiled=True,
    )


def solution(mesh):
    return jax.shard_map(
        body,
        mesh=mesh,
        in_specs=(P("seq", "tp"), P("seq", None), P("seq", None), P("tp", None)),
        out_specs=P(("seq", "tp"), None),
        check_vma=False,
    )
```

profile of v0, /device:TPU:22, one launch (start us, length us, event | category | flops | bytes accessed | tf_op | source)
XLA Modules:
  0.0 131.5 jit_solution(881336122191388604)
XLA Ops:
  6.5 1.0 constant_dynamic-slice_fusion.4
  7.8 1.9 %collective-permute-start = (bf16[1,2,256,256]{2,3,1,0:T(8,128)(2,1)S(1)}, bf16[1,2,256,256]{2,3,1,0:T(8,128)(2,1)S(1)}, u32[]{:S(2)}, u32[]{:S(2)}) collective-permute-start(bf16[1,2,256,256]{2,3,1,0:T(8,128)(2,1)S(1)} %maximum_bitcast_fusion), channel_id=1, source_target_pairs={{0,4},{4,8},{8,12},{12,16},{16,20},{20,24},{24,28},{1,5},{5,9},{9,... | collective-permute-start | bytes 786440 | tf_op jit(solution)/shard_map/ppermute | solution.py:15
  9.7 1.2 copy.17
  11.5 0.5 fusion.39
  12.0 3.4 %collective-permute-done = bf16[1,2,256,256]{2,3,1,0:T(8,128)(2,1)S(1)} collective-permute-done((bf16[1,2,256,256]{2,3,1,0:T(8,128)(2,1)S(1)}, bf16[1,2,256,256]{2,3,1,0:T(8,128)(2,1)S(1)}, u32[]{:S(2)}, u32[]{:S(2)}) %collective-permute-start) | collective-permute-done | bytes 262176 | tf_op jit(solution)/shard_map/ppermute | solution.py:15
  15.5 1.3 collective-permute-start.1
  16.8 0.5 fusion.40
  17.4 0.3 fusion.25
  17.7 0.3 fusion.27
  18.0 0.5 fusion.30
  18.6 0.5 fusion.28
  19.1 10.1 %collective-permute-done.1 = bf16[2,2,256,256]{2,3,1,0:T(8,128)(2,1)S(1)} collective-permute-done((bf16[2,2,256,256]{2,3,1,0:T(8,128)(2,1)S(1)}, bf16[2,2,256,256]{2,3,1,0:T(8,128)(2,1)S(1)}, u32[]{:S(2)}, u32[]{:S(2)}) %collective-permute-start.1) | collective-permute-done | bytes 524320 | tf_op jit(solution)/shard_map/ppermute | solution.py:15
  29.2 1.1 pad_maximum_fusion
  30.3 1.3 collective-permute-start.2
  31.6 3.7 %while.51 = (s32[]{:T(128)}, f32[256,2,4]{0,2,1:T(4,128)S(1)}, f32[256,2,4]{0,2,1:T(4,128)S(1)}, f32[256,2,4,128]{0,3,2,1:T(8,128)S(1)}, s32[]{:T(128)}, /*index...) while((s32[]{:T(128)}, f32[256,2,4]{0,2,1:T(4,128)S(1)}, ...), condition=%wide.region_7.8_spmd.clone.clone, body=%wide.region_4.7_spmd.clone.clone.sunk | while | flops 272839168 | bytes 9972413 | solution.py:78
  31.8 0.5 fusion.76
  32.7 0.7 fusion.78
  33.7 0.5 fusion.76
  34.6 0.7 fusion.78
  35.3 19.7 %collective-permute-done.2 = bf16[4,2,256,256]{2,3,1,0:T(8,128)(2,1)S(1)} collective-permute-done((bf16[4,2,256,256]{2,3,1,0:T(8,128)(2,1)}, bf16[4,2,256,256]{2,3,1,0:T(8,128)(2,1)S(1)}, u32[]{:S(2)}, u32[]{:S(2)}) %collective-permute-start.2) | collective-permute-done | bytes 1048608 | tf_op jit(solution)/shard_map/ppermute | solution.py:15
  55.0 7.4 %while.52 = (s32[]{:T(128)}, f32[256,2,4]{0,2,1:T(4,128)S(1)}, f32[256,2,4]{0,2,1:T(4,128)S(1)}, f32[256,2,4,128]{0,3,2,1:T(8,128)S(1)}, s32[]{:T(128)}, /*index...) while((s32[]{:T(128)}, f32[256,2,4]{0,2,1:T(4,128)S(1)}, ...), condition=%wide.region_11.12_spmd.clone.clone, body=%wide.region_8.11_spmd.clone.clone.sunk | while | flops 272839168 | bytes 9972413 | solution.py:78
  55.2 0.5 fusion.84
  56.1 0.7 fusion.86
  57.1 0.5 fusion.84
  58.0 0.7 fusion.86
  58.9 0.5 fusion.84
  59.8 0.7 fusion.86
  60.8 0.5 fusion.84
  61.4 0.3 fusion.85
  61.7 0.7 fusion.86
  62.5 8.3 %convolution_convert_fusion = bf16[256,5120]{1,0:T(8,128)(2,1)} fusion(bf16[256,1024]{0,1:T(8,128)(2,1)S(1)} %bitcast.163, bf16[1024,5120]{1,0:T(8,128)(2,1)} %param.11), kind=kOutput, calls=%fused_computation.56 | convolution fusion | flops 2685665280 | bytes 13631488 | tf_op jit(solution)/shard_map/dot_general | solution.py:86
  70.8 53.9 %reduce-scatter.2.cloned.1.call-done = bf16[64,5120]{1,0:T(8,128)(2,1)} async-done(((bf16[256,5120]{1,0:T(8,128)(2,1)}), bf16[64,5120]{1,0:T(8,128)(2,1)}) %reduce-scatter.2.cloned.1.call-update) | async-done | bytes 655376 | tf_op jit(solution)/shard_map/reduce_scatter | solution.py:85
  (73 shorter events, 3.9 us)
Async XLA Ops:
  6.5 118.1 %reduce-scatter.2.cloned.1.call-start = ((), (), s32[]{:S(2)}) async-start(), calls=%async_computation.1 | async-start | bytes 3276800 | tf_op jit(solution)/shard_map/reduce_scatter | solution.py:85
  7.8 7.7 %collective-permute-start = (bf16[1,2,256,256]{2,3,1,0:T(8,128)(2,1)S(1)}, bf16[1,2,256,256]{2,3,1,0:T(8,128)(2,1)S(1)}, u32[]{:S(2)}, u32[]{:S(2)}) collective-permute-start(bf16[1,2,256,256]{2,3,1,0:T(8,128)(2,1)S(1)} %maximum_bitcast_fusion), channel_id=1, source_target_pairs={{0,4},{4,8},{8,12},{12,16},{16,20},{20,24},{24,28},{1,5},{5,9},{9,... | collective-permute-start | bytes 786440 | tf_op jit(solution)/shard_map/ppermute | solution.py:15
  15.5 13.6 %collective-permute-start.1 = (bf16[2,2,256,256]{2,3,1,0:T(8,128)(2,1)S(1)}, bf16[2,2,256,256]{2,3,1,0:T(8,128)(2,1)S(1)}, u32[]{:S(2)}, u32[]{:S(2)}) collective-permute-start(bf16[2,2,256,256]{2,3,1,0:T(8,128)(2,1)S(1)} %pad_maximum_fusion.1), channel_id=1, source_target_pairs={{0,8},{4,12},{8,16},{12,20},{16,24},{20,28},{1,9},{5,13},{9,17},{1... | collective-permute-start | bytes 1572872 | tf_op jit(solution)/shard_map/ppermute | solution.py:15
  30.3 24.7 %collective-permute-start.2 = (bf16[4,2,256,256]{2,3,1,0:T(8,128)(2,1)}, bf16[4,2,256,256]{2,3,1,0:T(8,128)(2,1)S(1)}, u32[]{:S(2)}, u32[]{:S(2)}) collective-permute-start(bf16[4,2,256,256]{2,3,1,0:T(8,128)(2,1)} %pad_maximum_fusion), channel_id=1, source_target_pairs={{0,16},{4,20},{8,24},{12,28},{1,17},{5,21},{9,25},{13,29},{2,18},{... | collective-permute-start | bytes 3145736 | tf_op jit(solution)/shard_map/ppermute | solution.py:15
Sparse Core Ops, SparseCore 0:
  70.9 53.7 reduce-scatter.1
where the time goes:
time: 134 us; the launch traced here: 132 us
  waiting for transfers between devices  87.1 us (65%)
  matrix products  17.7 us (13%)
  between operations  13.5 us (10%)
  other arithmetic  5.22 us (4%)
  starting transfers between devices  4.49 us (3%)
  local copies, waits for them, and re-layouts  2.91 us (2%)
    reduce_scatter x1, waiting for transfers between devices, body(): lax.psum_scatter(jnp.dot(attended, out_weight, preferred_element_type=jnp...  53.9 us
    ppermute x3, waiting for transfers between devices, passed_along(): return lax.ppermute(block, axis, route)  33.2 us
    dot_general x1, matrix products, body(): jnp.dot(attended, out_weight, preferred_element_type=jnp.float32)  8.26 us
    dot_general x8, matrix products, fold_block(): jnp.einsum('tgrs,sgd->tgrd', weight.astype(jnp.bfloat16), v_rows, preferr...  5.13 us
    ppermute x3, starting transfers between devices, passed_along(): return lax.ppermute(block, axis, route)  4.49 us
    dot_general x8, matrix products, fold_block(): jnp.einsum('tgrd,sgd->tgrs', q_split, k_rows, preferred_element_type=jnp....  4.36 us
  transfers between devices with their start and end apart: 4, of which 4 were waited for; matrix products, arithmetic and copies ran while one was open for 6% of the time, Pallas kernels for 0%

commit v1 on v0

v1 whole, which is shorter than its diff:
```python
import functools
import math

import jax
import jax.numpy as jnp
from jax import lax
from jax.experimental import pallas as pl
from jax.experimental.pallas import tpu as pltpu
from jax.sharding import PartitionSpec as P

QUERY_HEADS = 32
KEY_VALUE_HEADS = 8
HEAD_DIMENSION = 128
STRETCH = 8192
LANES = 128
EXPONENT = HEAD_DIMENSION ** (-0.5) * math.log2(math.e)
NEGATIVE = -1e30
VMEM_LIMIT = 48 * 1024 * 1024


def dot_nt(a, b):
    return lax.dot_general(a, b, (((1,), (1,)), ((), ())), preferred_element_type=jnp.float32)


def spread(column):
    return jnp.broadcast_to(column, (column.shape[0], LANES))


def fold(q_ref, pairs, acc_ref, top_ref, total_ref, heads, per_kv):
    hd = HEAD_DIMENSION
    kv_here = heads // per_kv
    for h in range(heads):
        g = h // per_kv
        q = q_ref[:, h * hd : (h + 1) * hd]
        score = jnp.concatenate(
            [dot_nt(q, pair[:, g * hd : (g + 1) * hd]) for pair in pairs], axis=1
        )
        score = score * EXPONENT
        old = top_ref[h]
        new = jnp.maximum(old, spread(jnp.max(score, axis=1, keepdims=True)))
        shrink = jnp.exp2(old - new)
        weight = jnp.exp2(score - new[:, :1])
        total_ref[h] = total_ref[h] * shrink + spread(jnp.sum(weight, axis=1, keepdims=True))
        weight = weight.astype(jnp.bfloat16)
        mixed = None
        at = 0
        for pair in pairs:
            rows = pair.shape[0]
            part = jnp.dot(
                weight[:, at : at + rows],
                pair[:, (kv_here + g) * hd : (kv_here + g + 1) * hd],
                preferred_element_type=jnp.float32,
            )
            mixed = part if mixed is None else mixed + part
            at += rows
        acc_ref[h] = acc_ref[h] * shrink + mixed
        top_ref[h] = new


def own_kernel(flags, q_ref, own_ref, other_ref, acc_ref, top_ref, total_ref, *, heads, per_kv):
    hd = HEAD_DIMENSION
    kv_here = heads // per_kv
    tok = q_ref.shape[0]
    visible = lax.broadcasted_iota(jnp.int32, (tok, tok), 0) >= lax.broadcasted_iota(
        jnp.int32, (tok, tok), 1
    )
    for h in range(heads):
        g = h // per_kv
        score = dot_nt(q_ref[:, h * hd : (h + 1) * hd], own_ref[:, g * hd : (g + 1) * hd])
        score = jnp.where(visible, score * EXPONENT, NEGATIVE)
        top = jnp.max(score, axis=1, keepdims=True)
        weight = jnp.exp2(score - top)
        top_ref[h] = spread(top)
        total_ref[h] = spread(jnp.sum(weight, axis=1, keepdims=True))
        acc_ref[h] = jnp.dot(
            weight.astype(jnp.bfloat16),
            own_ref[:, (kv_here + g) * hd : (kv_here + g + 1) * hd],
            preferred_element_type=jnp.float32,
        )

    @pl.when(flags[0] > 0)
    def _():
        fold(q_ref, [other_ref], acc_ref, top_ref, total_ref, heads, per_kv)


def rest_kernel(flags, q_ref, acc_in, top_in, total_in, *refs, heads, per_kv, chips, chunks, tile):
    hd = HEAD_DIMENSION
    blocks, refs = refs[: 2 * chips], refs[2 * chips :]
    w_hbm, refs = refs[0], refs[1:]
    outs, refs = refs[:chunks], refs[chunks:]
    acc_ref, top_ref, total_ref, att_ref, w_ref, sems = refs
    tiles = w_hbm.shape[1] // tile
    copies = [
        pltpu.make_async_copy(
            w_hbm.at[:, pl.ds(i * tile, tile)], w_ref.at[:, pl.ds(i * tile, tile)], sems.at[i]
        )
        for i in range(tiles)
    ]
    for copy in copies:
        copy.start()
    acc_ref[...] = acc_in[...]
    top_ref[...] = top_in[...]
    total_ref[...] = total_in[...]
    for d in range(chips):

        @pl.when(flags[d] > 0)
        def _(d=d):
            pair = [blocks[2 * d], blocks[2 * d + 1]]
            fold(q_ref, pair, acc_ref, top_ref, total_ref, heads, per_kv)

    for h in range(heads):
        att_ref[:, h * hd : (h + 1) * hd] = (acc_ref[h] / total_ref[h]).astype(jnp.bfloat16)
    rows = q_ref.shape[0] // chunks
    order = [
        att_ref[pl.ds(pl.multiple_of(flags[chips + i] * rows, rows), rows), :]
        for i in range(chunks)
    ]
    attended = jnp.concatenate(order, axis=0)
    for i in range(tiles):
        copies[i].wait()
        cols = slice(i * tile, (i + 1) * tile)
        part = jnp.dot(attended, w_ref[:, cols], preferred_element_type=jnp.float32)
        for j in range(chunks):
            outs[j][:, cols] = part[j * rows : (j + 1) * rows].astype(jnp.bfloat16)


def whole_block(shape):
    return pl.BlockSpec(shape, lambda *_: (0,) * len(shape))


def added(*terms):
    total = terms[0].astype(jnp.float32)
    for term in terms[1:]:
        total = total + term.astype(jnp.float32)
    return total.astype(terms[0].dtype)


def body(queries, keys, values, out_weight):
    tok = queries.shape[0]
    hd = HEAD_DIMENSION
    heads = queries.shape[1] // hd
    group = QUERY_HEADS // KEY_VALUE_HEADS
    kv_here = max(1, heads // group)
    per_kv = heads // kv_here
    width = out_weight.shape[1]
    seq_devs, tp_devs = lax.axis_size("seq"), lax.axis_size("tp")
    seq_at, tp_at = lax.axis_index("seq"), lax.axis_index("tp")
    first = tp_at * heads // group * hd
    own = jnp.concatenate(
        [lax.dynamic_slice_in_dim(x, first, kv_here * hd, 1) for x in (keys, values)], axis=1
    )
    devs = min(STRETCH // tok, seq_devs)
    chips = devs // 2
    place = seq_at % devs
    chip, core = place // 2, place % 2

    swap = [(i, i ^ 1) for i in range(seq_devs)]
    blocks, valid = [], []
    for d in range(chips - 1, 0, -1):
        pairs = [(i, i ^ (2 * d)) for i in range(seq_devs) if i ^ (2 * d) > i]
        blocks.append(lax.ppermute(own, "seq", pairs))
        valid.append(((chip ^ d) < chip).astype(jnp.int32))
    other = lax.ppermute(own, "seq", swap)
    both = []
    for block in blocks:
        both += [block, lax.ppermute(block, "seq", swap)]

    state = [jax.ShapeDtypeStruct((heads, tok, LANES), jnp.float32)] * 3
    state_block = whole_block((heads, tok, LANES))
    pair_block = whole_block(own.shape)
    q_block = whole_block(queries.shape)
    acc, top, total = pl.pallas_call(
        functools.partial(own_kernel, heads=heads, per_kv=per_kv),
        grid_spec=pltpu.PrefetchScalarGridSpec(
            num_scalar_prefetch=1,
            grid=(1,),
            in_specs=[q_block, pair_block, pair_block],
            out_specs=[state_block] * 3,
        ),
        out_shape=state,
        compiler_params=pltpu.CompilerParams(vmem_limit_bytes=VMEM_LIMIT),
        cost_estimate=pl.CostEstimate(
            flops=8 * heads * tok * tok * hd, bytes_accessed=4 * 2**20, transcendentals=0
        ),
    )(core[None].astype(jnp.int32), queries, own, other)

    chunks = tp_devs if tp_devs == 4 else 1
    if chunks == 4:
        low = tp_at < 2
        order = [
            jnp.where(low, 3, 0),
            jnp.where(low, 2, 1),
            tp_at ^ 1,
            tp_at,
        ]
    else:
        order = [jnp.int32(0)]
    flags = jnp.stack(valid + [o.astype(jnp.int32) for o in order])
    rows = tok // chunks
    tile = 512
    parts = pl.pallas_call(
        functools.partial(
            rest_kernel, heads=heads, per_kv=per_kv, chips=chips - 1, chunks=chunks, tile=tile
        ),
        grid_spec=pltpu.PrefetchScalarGridSpec(
            num_scalar_prefetch=1,
            grid=(1,),
            in_specs=[q_block]
            + [state_block] * 3
            + [pair_block] * len(both)
            + [pl.BlockSpec(memory_space=pl.ANY)],
            out_specs=[whole_block((rows, width))] * chunks,
            scratch_shapes=[pltpu.VMEM((heads, tok, LANES), jnp.float32)] * 3
            + [
                pltpu.VMEM((tok, heads * hd), jnp.bfloat16),
                pltpu.VMEM(out_weight.shape, jnp.bfloat16),
                pltpu.SemaphoreType.DMA((width // tile,)),
            ],
        ),
        out_shape=[jax.ShapeDtypeStruct((rows, width), jnp.bfloat16)] * chunks,
        compiler_params=pltpu.CompilerParams(vmem_limit_bytes=VMEM_LIMIT),
        cost_estimate=pl.CostEstimate(
            flops=2 * tok * width * heads * hd, bytes_accessed=16 * 2**20, transcendentals=0
        ),
    )(flags, queries, acc, top, total, *both, out_weight)

    if chunks == 1:
        return lax.psum_scatter(parts[0], "tp", scatter_dimension=0, tiled=True)
    far, near, side, mine = parts
    inward, sides = [(0, 1), (3, 2)], [(0, 1), (1, 0), (2, 3), (3, 2)]
    half = rows // 2
    got_far = lax.ppermute(far, "tp", inward)
    got_near = [lax.ppermute(x, "tp", inward) for x in (near[:half], near[half:])]
    got_side = lax.ppermute(side, "tp", sides)
    across_far = lax.ppermute(added(got_far, far), "tp", [(1, 3), (2, 0)])
    across_near = [
        lax.ppermute(added(got, x), "tp", [(1, 2), (2, 1)])
        for got, x in zip(got_near, (near[:half], near[half:]))
    ]
    return added(mine, got_side, across_far, jnp.concatenate(across_near, axis=0))


def solution(mesh):
    return jax.shard_map(
        body,
        mesh=mesh,
        in_specs=(P("seq", "tp"), P("seq", None), P("seq", None), P("tp", None)),
        out_specs=P(("seq", "tp"), None),
        check_vma=False,
    )
```

time: 134 us -> 92.5 us (0.69)
  the two profiles are of different devices: /device:TPU:22 before, /device:TPU:15 now
where the time goes in v1:
time: 92.5 us; the launch traced here: 92.2 us
  waiting for transfers between devices  42.7 us (46%)
  Pallas kernels  22.4 us (24%)
  starting transfers between devices  21.3 us (23%)
  local copies, waits for them, and re-layouts  4.12 us (4%)
  other arithmetic  1.51 us (2%)
    pallas_call x1, Pallas kernels, body(): pl.pallas_call(functools.partial(rest_kernel, heads=heads, per_kv=per_kv,...  17.8 us
    ppermute x1, waiting for transfers between devices, body(): got_far = lax.ppermute(far, 'tp', inward)  12.5 us
    ppermute x2, waiting for transfers between devices, body(): lax.ppermute(x, 'tp', inward)  11.6 us
    ppermute x3, waiting for transfers between devices, body(): blocks.append(lax.ppermute(own, 'seq', pairs))  9.8 us
    ppermute x2, waiting for transfers between devices, body(): lax.ppermute(added(got, x), 'tp', [(1, 2), (2, 1)])  8.68 us
    ppermute x2, starting transfers between devices, body(): lax.ppermute(added(got, x), 'tp', [(1, 2), (2, 1)])  5.28 us
    pallas_call x1, Pallas kernels, body(): pl.pallas_call(functools.partial(own_kernel, heads=heads, per_kv=per_kv),...  4.64 us
    ppermute x3, starting transfers between devices, body(): blocks.append(lax.ppermute(own, 'seq', pairs))  3.88 us
  transfers between devices with their start and end apart: 14, of which 7 were waited for; matrix products, arithmetic and copies ran while one was open for 0% of the time, Pallas kernels for 5%

profile of v1, /device:TPU:15, one launch (start us, length us, event | category | flops | bytes accessed | tf_op | source)
XLA Modules:
  0.0 92.2 jit_solution(7661664681077411013)
XLA Ops:
  0.0 1.0 %constant_dynamic-slice_fusion = (bf16[256,256]{1,0:T(8,128)(2,1)S(1)}, bf16[256,256]{1,0:T(8,128)(2,1)S(1)}) fusion(bf16[256,1024]{1,0:T(8,128)(2,1)} %param.6, s32[]{:T(128)S(6)} %select_n.35, bf16[256,1024]{1,0:T(8,128)(2,1)} %param.5), kind=kLoop, calls=%fused_computation.5 | loop fusion | bytes 524292 | tf_op jit(solution)/shard_map/dynamic_slice | solution.py:150
  1.0 1.3 %collective-permute-start.5 = (bf16[256,512]{1,0:T(8,128)(2,1)S(1)}, bf16[256,512]{1,0:T(8,128)(2,1)S(1)}, u32[]{:S(2)}, u32[]{:S(2)}) collective-permute-start(bf16[256,512]{1,0:T(8,128)(2,1)S(1)} %pad_maximum_fusion.own_ref), channel_id=1, source_target_pairs={{0,8},{4,12},{16,24},{20,28},{1,9},{5,13},{17,25},{21,29},{2,10},{... | collective-permute-start | bytes 786440 | tf_op jit(solution)/shard_map/ppermute | solution.py:161
  2.3 1.3 %collective-permute-start.3 = (bf16[256,512]{1,0:T(8,128)(2,1)S(1)}, bf16[256,512]{1,0:T(8,128)(2,1)S(1)}, u32[]{:S(2)}, u32[]{:S(2)}) collective-permute-start(bf16[256,512]{1,0:T(8,128)(2,1)S(1)} %pad_maximum_fusion.own_ref), channel_id=1, source_target_pairs={{0,16},{4,20},{8,24},{12,28},{1,17},{5,21},{9,25},{13,29},{2,18},{... | collective-permute-start | bytes 786440 | tf_op jit(solution)/shard_map/ppermute | solution.py:161
  3.6 1.3 %collective-permute-start.1 = (bf16[256,512]{1,0:T(8,128)(2,1)S(1)}, bf16[256,512]{1,0:T(8,128)(2,1)S(1)}, u32[]{:S(2)}, u32[]{:S(2)}) collective-permute-start(bf16[256,512]{1,0:T(8,128)(2,1)S(1)} %pad_maximum_fusion.own_ref), channel_id=1, source_target_pairs={{0,24},{4,28},{8,16},{12,20},{1,25},{5,29},{9,17},{13,21},{2,26},{... | collective-permute-start | bytes 786440 | tf_op jit(solution)/shard_map/ppermute | solution.py:161
  4.9 0.7 collective-permute-start
  5.7 4.4 %collective-permute-done.5.refs_4_ = bf16[256,512]{1,0:T(8,128)(2,1)S(1)} collective-permute-done((bf16[256,512]{1,0:T(8,128)(2,1)S(1)}, bf16[256,512]{1,0:T(8,128)(2,1)S(1)}, u32[]{:S(2)}, u32[]{:S(2)}) %collective-permute-start.5) | collective-permute-done | bytes 262176 | tf_op jit(solution)/shard_map/ppermute | solution.py:161
  10.1 1.5 %collective-permute-start.6 = (bf16[256,512]{1,0:T(8,128)(2,1)S(1)}, bf16[256,512]{1,0:T(8,128)(2,1)S(1)}, u32[]{:S(2)}, u32[]{:S(2)}) collective-permute-start(bf16[256,512]{1,0:T(8,128)(2,1)S(1)} %collective-permute-done.5.refs_4_), channel_id=1, source_target_pairs={{0,4},{4,0},{8,12},{12,8},{16,20},{20,16},{24,28},{28,24},{1,5},{5... | collective-permute-start | bytes 786440 | tf_op jit(solution)/shard_map/ppermute | solution.py:166
  11.6 5.4 %collective-permute-done.3.refs_2_ = bf16[256,512]{1,0:T(8,128)(2,1)S(1)} collective-permute-done((bf16[256,512]{1,0:T(8,128)(2,1)S(1)}, bf16[256,512]{1,0:T(8,128)(2,1)S(1)}, u32[]{:S(2)}, u32[]{:S(2)}) %collective-permute-start.3) | collective-permute-done | bytes 262176 | tf_op jit(solution)/shard_map/ppermute | solution.py:161
  17.0 1.5 %collective-permute-start.4 = (bf16[256,512]{1,0:T(8,128)(2,1)S(1)}, bf16[256,512]{1,0:T(8,128)(2,1)S(1)}, u32[]{:S(2)}, u32[]{:S(2)}) collective-permute-start(bf16[256,512]{1,0:T(8,128)(2,1)S(1)} %collective-permute-done.3.refs_2_), channel_id=1, source_target_pairs={{0,4},{4,0},{8,12},{12,8},{16,20},{20,16},{24,28},{28,24},{1,5},{5... | collective-permute-start | bytes 786440 | tf_op jit(solution)/shard_map/ppermute | solution.py:166
  18.6 0.0 collective-permute-done.1.refs_0_
  18.6 0.0 collective-permute-start.2
  18.6 0.1 stack.43.flags
  18.7 1.0 %copy-done.2 = bf16[256,1024]{1,0:T(8,128)(2,1)S(1)} copy-done((bf16[256,1024]{1,0:T(8,128)(2,1)S(1)}, bf16[256,1024]{1,0:T(8,128)(2,1)}, u32[]{:S(2)}) %copy-start.2) | copy-done | bytes 524312
  19.7 4.6 %shard_map.46 = (f32[8,256,128]{2,1,0:T(8,128)S(1)}, f32[8,256,128]{2,1,0:T(8,128)S(1)}, f32[8,256,128]{2,1,0:T(8,128)S(1)}) custom-call(s32[1]{0:T(128)} %bitcast.7.flags, bf16[256,1024]{1,0:T(8,128)(2,1)S(1)} %copy-done.2, bf16[256,512]{1,0:T(8,128)(2,1)S(1)} %pad_maximum_fusion.own_ref, bf16[256,512]{1,0:T(8,128)(2,1)S(1)} %collective-permute-done.other_ref), custom_call_target="tpu_custom_call" | custom-call | flops 536870912 | bytes 4194304 | tf_op jit(solution)/shard_map/pallas_call | solution.py:172
  24.3 1.0 %copy-done = f32[8,256,128]{2,1,0:T(8,128)} copy-done((f32[8,256,128]{2,1,0:T(8,128)}, f32[8,256,128]{2,1,0:T(8,128)S(1)}, u32[]{:S(2)}) %copy-start) | copy-done | bytes 1048600
  25.3 1.0 %copy-done.1 = f32[8,256,128]{2,1,0:T(8,128)} copy-done((f32[8,256,128]{2,1,0:T(8,128)}, f32[8,256,128]{2,1,0:T(8,128)S(1)}, u32[]{:S(2)}) %copy-start.1) | copy-done | bytes 1048600
  26.3 17.8 %shard_map.47 = (bf16[64,5120]{1,0:T(8,128)(2,1)S(1)}, bf16[64,5120]{1,0:T(8,128)(2,1)S(1)}, bf16[64,5120]{1,0:T(8,128)(2,1)S(1)}, bf16[64,5120]{1,0:T(8,128)(2,1)S(1)}) custom-call(s32[7]{0:T(128)S(1)} %stack.43.flags, bf16[256,1024]{1,0:T(8,128)(2,1)S(1)} %copy-done.2, f32[8,256,128]{2,1,0:T(8,128)S(1)} %get-tuple-element.12.acc_in, ...), custom_call_target="tpu_custom_call" | custom-call | flops 2684354560 | bytes 16777216 | tf_op jit(solution)/shard_map/pallas_call | solution.py:201
  44.1 1.3 %collective-permute-start.8 = (bf16[64,5120]{1,0:T(8,128)(2,1)S(1)}, bf16[64,5120]{1,0:T(8,128)(2,1)S(1)}, u32[]{:S(2)}, u32[]{:S(2)}) collective-permute-start(bf16[64,5120]{1,0:T(8,128)(2,1)S(1)} %get-tuple-element.17), channel_id=1, source_target_pairs={{0,1},{3,2},{4,5},{7,6},{8,9},{11,10},{12,13},{15,14},{16,17},{19,... | collective-permute-start | bytes 1966088 | tf_op jit(solution)/shard_map/ppermute | solution.py:232
  45.5 1.3 %collective-permute-start.10 = (bf16[32,5120]{1,0:T(8,128)(2,1)S(1)}, bf16[32,5120]{1,0:T(8,128)(2,1)S(1)}, u32[]{:S(2)}, u32[]{:S(2)}) collective-permute-start(bf16[32,5120]{1,0:T(8,128)(2,1)S(1)} %get-tuple-element.21), channel_id=1, source_target_pairs={{0,1},{3,2},{4,5},{7,6},{8,9},{11,10},{12,13},{15,14},{16,17},{19,... | collective-permute-start | bytes 983048 | tf_op jit(solution)/shard_map/ppermute | solution.py:233
  46.8 1.3 %collective-permute-start.12 = (bf16[32,5120]{1,0:T(8,128)(2,1)S(1)}, bf16[32,5120]{1,0:T(8,128)(2,1)S(1)}, u32[]{:S(2)}, u32[]{:S(2)}) collective-permute-start(bf16[32,5120]{1,0:T(8,128)(2,1)S(1)} %get-tuple-element.22), channel_id=1, source_target_pairs={{0,1},{3,2},{4,5},{7,6},{8,9},{11,10},{12,13},{15,14},{16,17},{19,... | collective-permute-start | bytes 983048 | tf_op jit(solution)/shard_map/ppermute | solution.py:233
  48.1 2.2 %collective-permute-start.7 = (bf16[64,5120]{1,0:T(8,128)(2,1)S(1)}, bf16[64,5120]{1,0:T(8,128)(2,1)S(1)}, u32[]{:S(2)}, u32[]{:S(2)}) collective-permute-start(bf16[64,5120]{1,0:T(8,128)(2,1)S(1)} %get-tuple-element.16), channel_id=1, source_target_pairs={{0,1},{1,0},{2,3},{3,2},{4,5},{5,4},{6,7},{7,6},{8,9},{9,8},{10,11... | collective-permute-start | bytes 1966088 | tf_op jit(solution)/shard_map/ppermute | solution.py:234
  50.3 12.5 %collective-permute-done.8 = bf16[64,5120]{1,0:T(8,128)(2,1)S(1)} collective-permute-done((bf16[64,5120]{1,0:T(8,128)(2,1)S(1)}, bf16[64,5120]{1,0:T(8,128)(2,1)S(1)}, u32[]{:S(2)}, u32[]{:S(2)}) %collective-permute-start.8) | collective-permute-done | bytes 655392 | tf_op jit(solution)/shard_map/ppermute | solution.py:232
  62.8 0.2 add_convert_fusion.1
  63.0 2.2 %collective-permute-start.9 = (bf16[64,5120]{1,0:T(8,128)(2,1)S(1)}, bf16[64,5120]{1,0:T(8,128)(2,1)S(1)}, u32[]{:S(2)}, u32[]{:S(2)}) collective-permute-start(bf16[64,5120]{1,0:T(8,128)(2,1)S(1)} %add_convert_fusion.1), channel_id=1, source_target_pairs={{1,3},{2,0},{5,7},{6,4},{9,11},{10,8},{13,15},{14,12},{17,19},{18,... | collective-permute-start | bytes 1966088 | tf_op jit(solution)/shard_map/ppermute | solution.py:235
  65.2 4.6 %collective-permute-done.10 = bf16[32,5120]{1,0:T(8,128)(2,1)S(1)} collective-permute-done((bf16[32,5120]{1,0:T(8,128)(2,1)S(1)}, bf16[32,5120]{1,0:T(8,128)(2,1)S(1)}, u32[]{:S(2)}, u32[]{:S(2)}) %collective-permute-start.10) | collective-permute-done | bytes 327712 | tf_op jit(solution)/shard_map/ppermute | solution.py:233
  69.8 7.0 %collective-permute-done.12 = bf16[32,5120]{1,0:T(8,128)(2,1)S(1)} collective-permute-done((bf16[32,5120]{1,0:T(8,128)(2,1)S(1)}, bf16[32,5120]{1,0:T(8,128)(2,1)S(1)}, u32[]{:S(2)}, u32[]{:S(2)}) %collective-permute-start.12) | collective-permute-done | bytes 327712 | tf_op jit(solution)/shard_map/ppermute | solution.py:233
  76.9 0.2 add_convert_fusion.3
  77.0 3.2 %collective-permute-start.11 = (bf16[32,5120]{1,0:T(8,128)(2,1)S(1)}, bf16[32,5120]{1,0:T(8,128)(2,1)S(1)}, u32[]{:S(2)}, u32[]{:S(2)}) collective-permute-start(bf16[32,5120]{1,0:T(8,128)(2,1)S(1)} %get-tuple-element.19), channel_id=1, source_target_pairs={{1,2},{2,1},{5,6},{6,5},{9,10},{10,9},{13,14},{14,13},{17,18},{18,... | collective-permute-start | bytes 983048 | tf_op jit(solution)/shard_map/ppermute | solution.py:237
  80.2 2.1 %collective-permute-start.13 = (bf16[32,5120]{1,0:T(8,128)(2,1)S(1)}, bf16[32,5120]{1,0:T(8,128)(2,1)S(1)}, u32[]{:S(2)}, u32[]{:S(2)}) collective-permute-start(bf16[32,5120]{1,0:T(8,128)(2,1)S(1)} %get-tuple-element.20), channel_id=1, source_target_pairs={{1,2},{2,1},{5,6},{6,5},{9,10},{10,9},{13,14},{14,13},{17,18},{18,... | collective-permute-start | bytes 983048 | tf_op jit(solution)/shard_map/ppermute | solution.py:237
  82.3 5.2 %collective-permute-done.11 = bf16[32,5120]{1,0:T(8,128)(2,1)S(1)} collective-permute-done((bf16[32,5120]{1,0:T(8,128)(2,1)S(1)}, bf16[32,5120]{1,0:T(8,128)(2,1)S(1)}, u32[]{:S(2)}, u32[]{:S(2)}) %collective-permute-start.11) | collective-permute-done | bytes 327712 | tf_op jit(solution)/shard_map/ppermute | solution.py:237
  87.5 3.5 %collective-permute-done.13 = bf16[32,5120]{1,0:T(8,128)(2,1)S(1)} collective-permute-done((bf16[32,5120]{1,0:T(8,128)(2,1)S(1)}, bf16[32,5120]{1,0:T(8,128)(2,1)S(1)}, u32[]{:S(2)}, u32[]{:S(2)}) %collective-permute-start.13) | collective-permute-done | bytes 327712 | tf_op jit(solution)/shard_map/ppermute | solution.py:237
  91.0 1.2 %add_convert_fusion = bf16[64,5120]{1,0:T(8,128)(2,1)} fusion(bf16[64,5120]{1,0:T(8,128)(2,1)S(1)} %collective-permute-done.9, bf16[64,5120]{1,0:T(8,128)(2,1)S(1)} %collective-permute-done.7, bf16[64,5120]{1,0:T(8,128)(2,1)S(1)} %get-tuple-element.15, bf16[32,5120]{1,0:T(8,128)(2,1)S(1)} %collective-permute-done.13, ...), kind=kLoop, calls=%fused_computation | loop fusion | flops 3604480 | bytes 3276800 | tf_op jit(solution)/shard_map/convert_element_type | solution.py:135
  (11 shorter events, 0.1 us)
Async XLA Ops:
  1.0 9.1 %collective-permute-start.5 = (bf16[256,512]{1,0:T(8,128)(2,1)S(1)}, bf16[256,512]{1,0:T(8,128)(2,1)S(1)}, u32[]{:S(2)}, u32[]{:S(2)}) collective-permute-start(bf16[256,512]{1,0:T(8,128)(2,1)S(1)} %pad_maximum_fusion.own_ref), channel_id=1, source_target_pairs={{0,8},{4,12},{16,24},{20,28},{1,9},{5,13},{17,25},{21,29},{2,10},{... | collective-permute-start | bytes 786440 | tf_op jit(solution)/shard_map/ppermute | solution.py:161
  2.3 14.7 %collective-permute-start.3 = (bf16[256,512]{1,0:T(8,128)(2,1)S(1)}, bf16[256,512]{1,0:T(8,128)(2,1)S(1)}, u32[]{:S(2)}, u32[]{:S(2)}) collective-permute-start(bf16[256,512]{1,0:T(8,128)(2,1)S(1)} %pad_maximum_fusion.own_ref), channel_id=1, source_target_pairs={{0,16},{4,20},{8,24},{12,28},{1,17},{5,21},{9,25},{13,29},{2,18},{... | collective-permute-start | bytes 786440 | tf_op jit(solution)/shard_map/ppermute | solution.py:161
  3.6 14.9 %collective-permute-start.1 = (bf16[256,512]{1,0:T(8,128)(2,1)S(1)}, bf16[256,512]{1,0:T(8,128)(2,1)S(1)}, u32[]{:S(2)}, u32[]{:S(2)}) collective-permute-start(bf16[256,512]{1,0:T(8,128)(2,1)S(1)} %pad_maximum_fusion.own_ref), channel_id=1, source_target_pairs={{0,24},{4,28},{8,16},{12,20},{1,25},{5,29},{9,17},{13,21},{2,26},{... | collective-permute-start | bytes 786440 | tf_op jit(solution)/shard_map/ppermute | solution.py:161
  4.9 13.7 %collective-permute-start = (bf16[256,512]{1,0:T(8,128)(2,1)S(1)}, bf16[256,512]{1,0:T(8,128)(2,1)S(1)}, u32[]{:S(2)}, u32[]{:S(2)}) collective-permute-start(bf16[256,512]{1,0:T(8,128)(2,1)S(1)} %pad_maximum_fusion.own_ref), channel_id=1, source_target_pairs={{0,4},{4,0},{8,12},{12,8},{16,20},{20,16},{24,28},{28,24},{1,5},{5... | collective-permute-start | bytes 786440 | tf_op jit(solution)/shard_map/ppermute | solution.py:163
  10.1 16.2 %collective-permute-start.6 = (bf16[256,512]{1,0:T(8,128)(2,1)S(1)}, bf16[256,512]{1,0:T(8,128)(2,1)S(1)}, u32[]{:S(2)}, u32[]{:S(2)}) collective-permute-start(bf16[256,512]{1,0:T(8,128)(2,1)S(1)} %collective-permute-done.5.refs_4_), channel_id=1, source_target_pairs={{0,4},{4,0},{8,12},{12,8},{16,20},{20,16},{24,28},{28,24},{1,5},{5... | collective-permute-start | bytes 786440 | tf_op jit(solution)/shard_map/ppermute | solution.py:166
  17.0 9.3 %collective-permute-start.4 = (bf16[256,512]{1,0:T(8,128)(2,1)S(1)}, bf16[256,512]{1,0:T(8,128)(2,1)S(1)}, u32[]{:S(2)}, u32[]{:S(2)}) collective-permute-start(bf16[256,512]{1,0:T(8,128)(2,1)S(1)} %collective-permute-done.3.refs_2_), channel_id=1, source_target_pairs={{0,4},{4,0},{8,12},{12,8},{16,20},{20,16},{24,28},{28,24},{1,5},{5... | collective-permute-start | bytes 786440 | tf_op jit(solution)/shard_map/ppermute | solution.py:166
  18.6 7.8 %collective-permute-start.2 = (bf16[256,512]{1,0:T(8,128)(2,1)S(1)}, bf16[256,512]{1,0:T(8,128)(2,1)S(1)}, u32[]{:S(2)}, u32[]{:S(2)}) collective-permute-start(bf16[256,512]{1,0:T(8,128)(2,1)S(1)} %collective-permute-done.1.refs_0_), channel_id=1, source_target_pairs={{0,4},{4,0},{8,12},{12,8},{16,20},{20,16},{24,28},{28,24},{1,5},{5... | collective-permute-start | bytes 786440 | tf_op jit(solution)/shard_map/ppermute | solution.py:166
  18.6 1.0 %copy-start.2 = (bf16[256,1024]{1,0:T(8,128)(2,1)S(1)}, bf16[256,1024]{1,0:T(8,128)(2,1)}, u32[]{:S(2)}) copy-start(bf16[256,1024]{1,0:T(8,128)(2,1)} %q_ref.3) | copy-start | bytes 1572868
  24.3 1.0 %copy-start = (f32[8,256,128]{2,1,0:T(8,128)}, f32[8,256,128]{2,1,0:T(8,128)S(1)}, u32[]{:S(2)}) copy-start(f32[8,256,128]{2,1,0:T(8,128)S(1)} %get-tuple-element.13.top_in) | copy-start | bytes 3145732
  25.3 1.0 %copy-start.1 = (f32[8,256,128]{2,1,0:T(8,128)}, f32[8,256,128]{2,1,0:T(8,128)S(1)}, u32[]{:S(2)}) copy-start(f32[8,256,128]{2,1,0:T(8,128)S(1)} %get-tuple-element.14.total_in) | copy-start | bytes 3145732
  44.1 18.7 %collective-permute-start.8 = (bf16[64,5120]{1,0:T(8,128)(2,1)S(1)}, bf16[64,5120]{1,0:T(8,128)(2,1)S(1)}, u32[]{:S(2)}, u32[]{:S(2)}) collective-permute-start(bf16[64,5120]{1,0:T(8,128)(2,1)S(1)} %get-tuple-element.17), channel_id=1, source_target_pairs={{0,1},{3,2},{4,5},{7,6},{8,9},{11,10},{12,13},{15,14},{16,17},{19,... | collective-permute-start | bytes 1966088 | tf_op jit(solution)/shard_map/ppermute | solution.py:232
  45.5 24.4 %collective-permute-start.10 = (bf16[32,5120]{1,0:T(8,128)(2,1)S(1)}, bf16[32,5120]{1,0:T(8,128)(2,1)S(1)}, u32[]{:S(2)}, u32[]{:S(2)}) collective-permute-start(bf16[32,5120]{1,0:T(8,128)(2,1)S(1)} %get-tuple-element.21), channel_id=1, source_target_pairs={{0,1},{3,2},{4,5},{7,6},{8,9},{11,10},{12,13},{15,14},{16,17},{19,... | collective-permute-start | bytes 983048 | tf_op jit(solution)/shard_map/ppermute | solution.py:233
  46.8 30.1 %collective-permute-start.12 = (bf16[32,5120]{1,0:T(8,128)(2,1)S(1)}, bf16[32,5120]{1,0:T(8,128)(2,1)S(1)}, u32[]{:S(2)}, u32[]{:S(2)}) collective-permute-start(bf16[32,5120]{1,0:T(8,128)(2,1)S(1)} %get-tuple-element.22), channel_id=1, source_target_pairs={{0,1},{3,2},{4,5},{7,6},{8,9},{11,10},{12,13},{15,14},{16,17},{19,... | collective-permute-start | bytes 983048 | tf_op jit(solution)/shard_map/ppermute | solution.py:233
  48.1 43.0 %collective-permute-start.7 = (bf16[64,5120]{1,0:T(8,128)(2,1)S(1)}, bf16[64,5120]{1,0:T(8,128)(2,1)S(1)}, u32[]{:S(2)}, u32[]{:S(2)}) collective-permute-start(bf16[64,5120]{1,0:T(8,128)(2,1)S(1)} %get-tuple-element.16), channel_id=1, source_target_pairs={{0,1},{1,0},{2,3},{3,2},{4,5},{5,4},{6,7},{7,6},{8,9},{9,8},{10,11... | collective-permute-start | bytes 1966088 | tf_op jit(solution)/shard_map/ppermute | solution.py:234
  63.0 28.0 %collective-permute-start.9 = (bf16[64,5120]{1,0:T(8,128)(2,1)S(1)}, bf16[64,5120]{1,0:T(8,128)(2,1)S(1)}, u32[]{:S(2)}, u32[]{:S(2)}) collective-permute-start(bf16[64,5120]{1,0:T(8,128)(2,1)S(1)} %add_convert_fusion.1), channel_id=1, source_target_pairs={{1,3},{2,0},{5,7},{6,4},{9,11},{10,8},{13,15},{14,12},{17,19},{18,... | collective-permute-start | bytes 1966088 | tf_op jit(solution)/shard_map/ppermute | solution.py:235
  77.0 10.5 %collective-permute-start.11 = (bf16[32,5120]{1,0:T(8,128)(2,1)S(1)}, bf16[32,5120]{1,0:T(8,128)(2,1)S(1)}, u32[]{:S(2)}, u32[]{:S(2)}) collective-permute-start(bf16[32,5120]{1,0:T(8,128)(2,1)S(1)} %get-tuple-element.19), channel_id=1, source_target_pairs={{1,2},{2,1},{5,6},{6,5},{9,10},{10,9},{13,14},{14,13},{17,18},{18,... | collective-permute-start | bytes 983048 | tf_op jit(solution)/shard_map/ppermute | solution.py:237
  80.2 10.8 %collective-permute-start.13 = (bf16[32,5120]{1,0:T(8,128)(2,1)S(1)}, bf16[32,5120]{1,0:T(8,128)(2,1)S(1)}, u32[]{:S(2)}, u32[]{:S(2)}) collective-permute-start(bf16[32,5120]{1,0:T(8,128)(2,1)S(1)} %get-tuple-element.20), channel_id=1, source_target_pairs={{1,2},{2,1},{5,6},{6,5},{9,10},{10,9},{13,14},{14,13},{17,18},{18,... | collective-permute-start | bytes 983048 | tf_op jit(solution)/shard_map/ppermute | solution.py:237

commit v2 on v0

v2 whole, which is shorter than its diff:
```python
import functools
import math

import jax
import jax.numpy as jnp
from jax import lax
from jax.experimental import pallas as pl
from jax.experimental.pallas import tpu as pltpu
from jax.sharding import PartitionSpec as P

QUERY_HEADS = 32
KEY_VALUE_HEADS = 8
HEAD_DIMENSION = 128
STRETCH = 8192
EXPONENT = HEAD_DIMENSION ** (-0.5) * math.log2(math.e)
NEGATIVE = -1e30
TILE = 512


def dot(a, b):
    return jnp.dot(a, b, preferred_element_type=jnp.float32)


def dot_nt(a, b):
    return lax.dot_general(a, b, (((1,), (1,)), ((), ())), preferred_element_type=jnp.float32)


def head(index):
    return slice(index * HEAD_DIMENSION, (index + 1) * HEAD_DIMENSION)


def spread(column):
    return jnp.broadcast_to(column, (column.shape[0], HEAD_DIMENSION))


def keys_of(first, second, g):
    return jnp.concatenate([first[:, head(g)], second[:, head(g)]], axis=0)


def values_of(first, second, g, kv_here):
    values = keys_of(first, second, kv_here + g)
    return jnp.concatenate([values, jnp.ones_like(values)], axis=1)


def folded(query, keys, values, acc, top):
    score = dot_nt(query, keys)
    new = jnp.maximum(top, spread(jnp.max(score, axis=1, keepdims=True)))
    shrink = jnp.exp2((top - new) * EXPONENT)
    weight = jnp.exp2((score - new[:, :1]) * EXPONENT).astype(jnp.bfloat16)
    return acc * jnp.concatenate([shrink, shrink], axis=1) + dot(weight, values), new


def fetch(pairs, sems):
    copies = [pltpu.make_async_copy(src, dst, sems.at[i]) for i, (src, dst) in enumerate(pairs)]
    for copy in copies:
        copy.start()
    return copies


def pack_kernel(keys, values, own_ref, sems, *, per_kv, heads):
    half = own_ref.shape[1] // 2
    at = lax.axis_index("tp")
    if heads < per_kv:
        at = lax.div(at, per_kv // heads)
    cols = pl.ds(pl.multiple_of(at * half, HEAD_DIMENSION), half)
    for copy in fetch(
        [(keys.at[:, cols], own_ref.at[:, :half]), (values.at[:, cols], own_ref.at[:, half:])], sems
    ):
        copy.wait()


def stage_kernel(*refs):
    half = (len(refs) - 1) // 2
    for copy in fetch(list(zip(refs[:half], refs[half : 2 * half])), refs[-1]):
        copy.wait()


def layer_kernel(q_ref, *refs, heads, per_kv, chips, order):
    chunks = len(order)
    kv_ref, refs = refs[: 2 * chips], refs[2 * chips :]
    w_ref, outs, refs = refs[0], refs[1 : 1 + chunks], refs[1 + chunks :]
    acc_ref, top_ref, att_ref = refs
    rows = outs[0].shape[0]
    tok = kv_ref[0].shape[0]
    kv_here = heads // per_kv
    place = lax.rem(lax.axis_index("seq"), 2 * chips)
    chip, core = lax.div(place, 2), lax.rem(place, 2)
    tp_at = lax.axis_index("tp")
    starts = [pl.multiple_of(chunk(tp_at) * rows, rows) for chunk in order]
    there = [pl.ds(start, rows) for start in starts]
    here = [slice(i * rows, (i + 1) * rows) for i in range(chunks)]

    def every(step):
        for i in range(chunks):
            for g in range(kv_here):
                mine = range(g * per_kv, (g + 1) * per_kv)
                step(i, g, jnp.concatenate([q_ref[there[i], head(h)] for h in mine], axis=0))

    def own(i, g, query):
        score = dot_nt(query, keys_of(kv_ref[0], kv_ref[1], g))
        row = lax.broadcasted_iota(jnp.int32, score.shape, 0) % rows + starts[i]
        col = lax.broadcasted_iota(jnp.int32, score.shape, 1)
        score = jnp.where(col <= jnp.where(col < tok, row, core * 2 * tok), score, NEGATIVE)
        top = jnp.max(score, axis=1, keepdims=True)
        weight = jnp.exp2((score - top) * EXPONENT).astype(jnp.bfloat16)
        acc_ref[i, g] = dot(weight, values_of(kv_ref[0], kv_ref[1], g, kv_here))
        top_ref[i, g] = spread(top)

    def others(i, g, query, pair=None):
        acc_ref[i, g], top_ref[i, g] = folded(
            query,
            keys_of(*pair, g),
            values_of(*pair, g, kv_here),
            acc_ref[i, g],
            top_ref[i, g],
        )

    for d in range(chips):
        if d == 0:
            every(own)
        else:
            pair = (kv_ref[2 * d], kv_ref[2 * d + 1])
            pl.when((chip ^ d) < chip)(
                functools.partial(every, functools.partial(others, pair=pair))
            )
    for i in range(chunks):
        for h in range(heads):
            g, j = h // per_kv, h % per_kv
            state = acc_ref[i, g, j * rows : (j + 1) * rows, :]
            att_ref[here[i], head(h)] = (
                state[:, :HEAD_DIMENSION] / state[:, HEAD_DIMENSION:]
            ).astype(jnp.bfloat16)
    attended = att_ref[...]
    for at in range(0, w_ref.shape[1], TILE):
        part = dot(attended, w_ref[:, at : at + TILE]).astype(jnp.bfloat16)
        for i in range(chunks):
            outs[i][:, at : at + TILE] = part[here[i]]


def call(kernel, out_shape, *args, scratch, limit, place=pltpu.VMEM):
    return pl.pallas_call(
        kernel,
        out_shape=out_shape,
        in_specs=[pl.BlockSpec(memory_space=place)] * len(args),
        out_specs=[pl.BlockSpec(memory_space=pltpu.VMEM)] * len(out_shape),
        scratch_shapes=scratch,
        compiler_params=pltpu.CompilerParams(vmem_limit_bytes=limit * 2**20),
    )(*args)


def after(value, *others):
    return lax.optimization_barrier((value, *others))[0]


def added(*terms):
    total = terms[0].astype(jnp.float32)
    for term in terms[1:]:
        total = total + term.astype(jnp.float32)
    return total.astype(terms[0].dtype)


def body(queries, keys, values, out_weight):
    tok = queries.shape[0]
    hd = HEAD_DIMENSION
    heads = queries.shape[1] // hd
    group = QUERY_HEADS // KEY_VALUE_HEADS
    kv_here = max(1, heads // group)
    per_kv = heads // kv_here
    width = out_weight.shape[1]
    seq_devs, tp_devs = lax.axis_size("seq"), lax.axis_size("tp")
    pair_shape = (tok, 2 * kv_here * hd)
    semaphores = pltpu.SemaphoreType.DMA
    (own,) = call(
        functools.partial(pack_kernel, per_kv=group, heads=heads),
        [jax.ShapeDtypeStruct(pair_shape, keys.dtype)],
        keys,
        values,
        scratch=[semaphores((2,))],
        limit=56,
        place=pl.ANY,
    )
    devs = min(STRETCH // tok, seq_devs)
    chips = devs // 2

    swap = [(i, i ^ 1) for i in range(seq_devs)]
    blocks = [own]
    for d in range(1, chips):
        pairs = [(i, i ^ (2 * d)) for i in range(seq_devs) if i ^ (2 * d) > i]
        blocks.append(lax.ppermute(own, "seq", pairs))
    q_here, w_here = call(
        stage_kernel,
        [jax.ShapeDtypeStruct(x.shape, x.dtype) for x in (queries, out_weight)],
        queries,
        out_weight,
        scratch=[semaphores((2,))],
        limit=24,
        place=pl.ANY,
    )
    blocks[1:] = lax.optimization_barrier((*blocks[1:], q_here, w_here))[: chips - 1]
    both = []
    for block in blocks:
        both += [block, lax.ppermute(block, "seq", swap)]

    def layer(order, rows):
        chunks = len(order)
        return call(
            functools.partial(layer_kernel, heads=heads, per_kv=per_kv, chips=chips, order=order),
            [jax.ShapeDtypeStruct((rows, width), jnp.bfloat16)] * chunks,
            q_here,
            *both,
            w_here,
            scratch=[
                pltpu.VMEM((chunks, kv_here, per_kv * rows, 2 * hd), jnp.float32),
                pltpu.VMEM((chunks, kv_here, per_kv * rows, hd), jnp.float32),
                pltpu.VMEM((rows * chunks, heads * hd), jnp.bfloat16),
            ],
            limit=24,
        )

    if tp_devs != 4:
        (part,) = layer([lambda at: 0], tok)
        return lax.psum_scatter(part, "tp", scatter_dimension=0, tiled=True)

    rows = tok // 4
    (far,) = layer([lambda at: jnp.where(at < 2, 3, 0)], rows)
    inward, sides = [(0, 1), (3, 2)], [(0, 1), (1, 0), (2, 3), (3, 2)]
    got_far = lax.ppermute(far, "tp", inward)
    near, side, mine = layer(
        [lambda at: jnp.where(at < 2, 2, 1), lambda at: at ^ 1, lambda at: at], rows
    )
    halves = [near[: rows // 2], near[rows // 2 :]]
    got_near = [lax.ppermute(x, "tp", inward) for x in halves]
    got_side = lax.ppermute(side, "tp", sides)
    last = added(got_far, far)
    across = [lax.ppermute(last, "tp", [(1, 3), (2, 0)])]
    for got, x in zip(got_near, halves):
        last = added(after(got, last), x)
        across.append(lax.ppermute(last, "tp", [(1, 2), (2, 1)]))
    return added(mine, got_side, across[0], jnp.concatenate(across[1:], axis=0))


def solution(mesh):
    return jax.shard_map(
        body,
        mesh=mesh,
        in_specs=(P("seq", "tp"), P("seq", None), P("seq", None), P("tp", None)),
        out_specs=P(("seq", "tp"), None),
        check_vma=False,
    )
```

time: 134 us -> 78.2 us (0.58); the launches traced: 132 us -> 77.9 us
  waiting for transfers between devices: 87.1 us -> 36.8 us
  matrix products: 17.7 us -> 0 us
  Pallas kernels: 0 us -> 17.1 us
  starting transfers between devices: 4.49 us -> 18.3 us
  between operations: 13.5 us -> 0.16 us
  other arithmetic: 5.22 us -> 1.47 us
    reduce_scatter x1 -> x0, waiting for transfers between devices: 53.9 us -> none  [body(): lax.psum_scatter(jnp.dot(attended, out_weight, preferred_element_type=jnp...]
    dot_general x17 -> x0, matrix products: 17.7 us -> none  [the longest x1 8.26 us: body(): jnp.dot(attended, out_weight, preferred_element_type=jnp.float32)]
    pallas_call x0 -> x4, Pallas kernels: none -> 17.1 us  [call(): pl.pallas_call(kernel, out_shape=out_shape, in_specs=[pl.BlockSpec(memory...]
    ppermute x3 -> x14, starting transfers between devices: 4.49 us -> 18.3 us  [the longest x2 5.84 us: body(): across.append(lax.ppermute(last, 'tp', [(1, 2), (2, 1)]))]
    ppermute x3 -> x14, waiting for transfers between devices: 33.2 us -> 36.8 us  [the longest x2 12.4 us: body(): got_near = [lax.ppermute(x, 'tp', inward) for x in halves]]
    reduce_sum x8 -> x0, other arithmetic: 2.43 us -> none  [fold_block(): total = total * shrink + jnp.sum(weight, axis=3)]
    unnamed x3 -> x6, local copies, waits for them, and re-layouts: 1.62 us -> 3.98 us
    convert_element_type x1 -> x4, other arithmetic: 0.1 us -> 1.47 us  [added(): return total.astype(terms[0].dtype)]
  transfers between devices with their start and end apart: 4 -> 14, of which waited for: 4 -> 10; matrix products, arithmetic and copies ran while one was open for 6% -> 0% of each run, Pallas kernels for 0% -> 13%
where the time goes in v2:
time: 78.2 us; the launch traced here: 77.9 us
  waiting for transfers between devices  36.8 us (47%)
  starting transfers between devices  18.3 us (23%)
  Pallas kernels  17.1 us (22%)
  local copies, waits for them, and re-layouts  4.03 us (5%)
  other arithmetic  1.47 us (2%)
    pallas_call x4, Pallas kernels, call(): pl.pallas_call(kernel, out_shape=out_shape, in_specs=[pl.BlockSpec(memory...  17.1 us
    ppermute x2, waiting for transfers between devices, body(): got_near = [lax.ppermute(x, 'tp', inward) for x in halves]  12.4 us
    ppermute x3, waiting for transfers between devices, body(): blocks.append(lax.ppermute(own, 'seq', pairs))  7.94 us
    ppermute x1, waiting for transfers between devices, body(): got_side = lax.ppermute(side, 'tp', sides)  7.3 us
    ppermute x2, starting transfers between devices, body(): across.append(lax.ppermute(last, 'tp', [(1, 2), (2, 1)]))  5.84 us
    unnamed x6, local copies, waits for them, and re-layouts  3.98 us
    ppermute x3, starting transfers between devices, body(): blocks.append(lax.ppermute(own, 'seq', pairs))  3.88 us
    ppermute x2, waiting for transfers between devices, body(): across.append(lax.ppermute(last, 'tp', [(1, 2), (2, 1)]))  3.88 us
  transfers between devices with their start and end apart: 14, of which 10 were waited for; matrix products, arithmetic and copies ran while one was open for 0% of the time, Pallas kernels for 13%

profile of v2, /device:TPU:22, one launch (start us, length us, event | category | flops | bytes accessed | tf_op | source)
XLA Modules:
  0.0 77.9 jit_solution(10160346985132122276)
XLA Ops:
  0.0 1.7 %shard_map.47.refs_0_ = bf16[256,512]{1,0:T(8,128)(2,1)} custom-call(bf16[256,1024]{1,0:T(8,128)(2,1)} %keys.1, bf16[256,1024]{1,0:T(8,128)(2,1)} %values.1), custom_call_target="tpu_custom_call" | custom-call | tf_op jit(solution)/shard_map/pallas_call | solution.py:141
  1.8 1.3 %collective-permute-start.3 = (bf16[256,512]{1,0:T(8,128)(2,1)}, bf16[256,512]{1,0:T(8,128)(2,1)S(1)}, u32[]{:S(2)}, u32[]{:S(2)}) collective-permute-start(bf16[256,512]{1,0:T(8,128)(2,1)} %shard_map.47.refs_0_), channel_id=1, source_target_pairs={{0,24},{4,28},{8,16},{12,20},{1,25},{5,29},{9,17},{13,21},{2,26},{... | collective-permute-start | bytes 786440 | tf_op jit(solution)/shard_map/ppermute | solution.py:189
  3.1 1.3 %collective-permute-start.2 = (bf16[256,512]{1,0:T(8,128)(2,1)}, bf16[256,512]{1,0:T(8,128)(2,1)S(1)}, u32[]{:S(2)}, u32[]{:S(2)}) collective-permute-start(bf16[256,512]{1,0:T(8,128)(2,1)} %shard_map.47.refs_0_), channel_id=1, source_target_pairs={{0,16},{4,20},{8,24},{12,28},{1,17},{5,21},{9,25},{13,29},{2,18},{... | collective-permute-start | bytes 786440 | tf_op jit(solution)/shard_map/ppermute | solution.py:189
  4.4 1.3 %collective-permute-start.1 = (bf16[256,512]{1,0:T(8,128)(2,1)}, bf16[256,512]{1,0:T(8,128)(2,1)S(1)}, u32[]{:S(2)}, u32[]{:S(2)}) collective-permute-start(bf16[256,512]{1,0:T(8,128)(2,1)} %shard_map.47.refs_0_), channel_id=1, source_target_pairs={{0,8},{4,12},{16,24},{20,28},{1,9},{5,13},{17,25},{21,29},{2,10},{... | collective-permute-start | bytes 786440 | tf_op jit(solution)/shard_map/ppermute | solution.py:189
  5.7 0.1 collective-permute-start
  5.8 4.0 %copy-done = bf16[1024,5120]{1,0:T(8,128)(2,1)S(1)} copy-done((bf16[1024,5120]{1,0:T(8,128)(2,1)S(1)}, bf16[1024,5120]{1,0:T(8,128)(2,1)}, u32[]{:S(2)}) %copy-start) | copy-done | bytes 10485784
  9.7 0.8 shard_map.46
  10.5 3.5 %collective-permute-done.3.refs_6_ = bf16[256,512]{1,0:T(8,128)(2,1)S(1)} collective-permute-done((bf16[256,512]{1,0:T(8,128)(2,1)}, bf16[256,512]{1,0:T(8,128)(2,1)S(1)}, u32[]{:S(2)}, u32[]{:S(2)}) %collective-permute-start.3) | collective-permute-done | bytes 262176 | tf_op jit(solution)/shard_map/ppermute | solution.py:189
  14.0 4.4 %collective-permute-done.2.refs_4_ = bf16[256,512]{1,0:T(8,128)(2,1)S(1)} collective-permute-done((bf16[256,512]{1,0:T(8,128)(2,1)}, bf16[256,512]{1,0:T(8,128)(2,1)S(1)}, u32[]{:S(2)}, u32[]{:S(2)}) %collective-permute-start.2) | collective-permute-done | bytes 262176 | tf_op jit(solution)/shard_map/ppermute | solution.py:189
  18.4 0.0 collective-permute-start.4
  18.4 0.5 collective-permute-start.5
  19.0 1.0 %collective-permute-done.4.refs_3_ = bf16[256,512]{1,0:T(8,128)(2,1)S(1)} collective-permute-done((bf16[256,512]{1,0:T(8,128)(2,1)S(1)}, bf16[256,512]{1,0:T(8,128)(2,1)S(1)}, u32[]{:S(2)}, u32[]{:S(2)}) %collective-permute-start.4) | collective-permute-done | bytes 262176 | tf_op jit(solution)/shard_map/ppermute | solution.py:202
  20.0 0.4 collective-permute-done.5.refs_5_
  20.3 0.4 collective-permute-done.6.refs_7_
  20.7 5.4 %shard_map.49 = bf16[64,5120]{1,0:T(8,128)(2,1)S(1)} custom-call(bf16[256,1024]{1,0:T(8,128)(2,1)S(1)} %get-tuple-element.15.q_ref, bf16[256,512]{1,0:T(8,128)(2,1)S(1)} %copy-done.1, bf16[256,512]{1,0:T(8,128)(2,1)S(1)} %collective-permute-done.refs_1_, bf16[256,512]{1,0:T(8,128)(2,1)S(1)} %collective-permute-done.1.refs_2_, ...), custom_call_target="tpu_custom_call" | custom-call | tf_op jit(solution)/shard_map/pallas_call | solution.py:141
  26.1 1.3 %collective-permute-start.8 = (bf16[64,5120]{1,0:T(8,128)(2,1)S(1)}, bf16[64,5120]{1,0:T(8,128)(2,1)S(1)}, u32[]{:S(2)}, u32[]{:S(2)}) collective-permute-start(bf16[64,5120]{1,0:T(8,128)(2,1)S(1)} %shard_map.49), channel_id=1, source_target_pairs={{0,1},{3,2},{4,5},{7,6},{8,9},{11,10},{12,13},{15,14},{16,17},{19,... | collective-permute-start | bytes 1966088 | tf_op jit(solution)/shard_map/ppermute | solution.py:227
  27.4 9.2 %shard_map.48 = (bf16[64,5120]{1,0:T(8,128)(2,1)S(1)}, bf16[64,5120]{1,0:T(8,128)(2,1)S(1)}, bf16[64,5120]{1,0:T(8,128)(2,1)S(1)}) custom-call(bf16[256,1024]{1,0:T(8,128)(2,1)S(1)} %get-tuple-element.15.q_ref, bf16[256,512]{1,0:T(8,128)(2,1)S(1)} %copy-done.1, bf16[256,512]{1,0:T(8,128)(2,1)S(1)} %collective-permute-done.refs_1_, ...), custom_call_target="tpu_custom_call" | custom-call | tf_op jit(solution)/shard_map/pallas_call | solution.py:141
  36.7 1.3 %collective-permute-start.10 = (bf16[32,5120]{1,0:T(8,128)(2,1)S(1)}, bf16[32,5120]{1,0:T(8,128)(2,1)S(1)}, u32[]{:S(2)}, u32[]{:S(2)}) collective-permute-start(bf16[32,5120]{1,0:T(8,128)(2,1)S(1)} %get-tuple-element.25), channel_id=1, source_target_pairs={{0,1},{3,2},{4,5},{7,6},{8,9},{11,10},{12,13},{15,14},{16,17},{19,... | collective-permute-start | bytes 983048 | tf_op jit(solution)/shard_map/ppermute | solution.py:232
  38.0 1.3 %collective-permute-start.12 = (bf16[32,5120]{1,0:T(8,128)(2,1)S(1)}, bf16[32,5120]{1,0:T(8,128)(2,1)S(1)}, u32[]{:S(2)}, u32[]{:S(2)}) collective-permute-start(bf16[32,5120]{1,0:T(8,128)(2,1)S(1)} %get-tuple-element.26), channel_id=1, source_target_pairs={{0,1},{3,2},{4,5},{7,6},{8,9},{11,10},{12,13},{15,14},{16,17},{19,... | collective-permute-start | bytes 983048 | tf_op jit(solution)/shard_map/ppermute | solution.py:232
  39.3 2.8 %collective-permute-start.7 = (bf16[64,5120]{1,0:T(8,128)(2,1)S(1)}, bf16[64,5120]{1,0:T(8,128)(2,1)S(1)}, u32[]{:S(2)}, u32[]{:S(2)}) collective-permute-start(bf16[64,5120]{1,0:T(8,128)(2,1)S(1)} %get-tuple-element.21), channel_id=1, source_target_pairs={{0,1},{1,0},{2,3},{3,2},{4,5},{5,4},{6,7},{7,6},{8,9},{9,8},{10,11... | collective-permute-start | bytes 1966088 | tf_op jit(solution)/shard_map/ppermute | solution.py:233
  42.0 3.5 %collective-permute-done.8 = bf16[64,5120]{1,0:T(8,128)(2,1)S(1)} collective-permute-done((bf16[64,5120]{1,0:T(8,128)(2,1)S(1)}, bf16[64,5120]{1,0:T(8,128)(2,1)S(1)}, u32[]{:S(2)}, u32[]{:S(2)}) %collective-permute-start.8) | collective-permute-done | bytes 655392 | tf_op jit(solution)/shard_map/ppermute | solution.py:227
  45.6 0.2 add_convert_fusion.1
  45.7 1.4 %collective-permute-start.9 = (bf16[64,5120]{1,0:T(8,128)(2,1)S(1)}, bf16[64,5120]{1,0:T(8,128)(2,1)S(1)}, u32[]{:S(2)}, u32[]{:S(2)}) collective-permute-start(bf16[64,5120]{1,0:T(8,128)(2,1)S(1)} %add_convert_fusion.1), channel_id=1, source_target_pairs={{1,3},{2,0},{5,7},{6,4},{9,11},{10,8},{13,15},{14,12},{17,19},{18,... | collective-permute-start | bytes 1966088 | tf_op jit(solution)/shard_map/ppermute | solution.py:235
  47.1 5.5 %collective-permute-done.10 = bf16[32,5120]{1,0:T(8,128)(2,1)S(1)} collective-permute-done((bf16[32,5120]{1,0:T(8,128)(2,1)S(1)}, bf16[32,5120]{1,0:T(8,128)(2,1)S(1)}, u32[]{:S(2)}, u32[]{:S(2)}) %collective-permute-start.10) | collective-permute-done | bytes 327712 | tf_op jit(solution)/shard_map/ppermute | solution.py:232
  52.6 0.1 add_convert_fusion.3
  52.7 6.9 %collective-permute-done.12 = bf16[32,5120]{1,0:T(8,128)(2,1)S(1)} collective-permute-done((bf16[32,5120]{1,0:T(8,128)(2,1)S(1)}, bf16[32,5120]{1,0:T(8,128)(2,1)S(1)}, u32[]{:S(2)}, u32[]{:S(2)}) %collective-permute-start.12) | collective-permute-done | bytes 327712 | tf_op jit(solution)/shard_map/ppermute | solution.py:232
  59.6 0.1 add_convert_fusion.2
  59.7 2.4 %collective-permute-start.13 = (bf16[32,5120]{1,0:T(8,128)(2,1)S(1)}, bf16[32,5120]{1,0:T(8,128)(2,1)S(1)}, u32[]{:S(2)}, u32[]{:S(2)}) collective-permute-start(bf16[32,5120]{1,0:T(8,128)(2,1)S(1)} %add_convert_fusion.2), channel_id=1, source_target_pairs={{1,2},{2,1},{5,6},{6,5},{9,10},{10,9},{13,14},{14,13},{17,18},{18,... | collective-permute-start | bytes 983048 | tf_op jit(solution)/shard_map/ppermute | solution.py:238
  62.1 3.5 %collective-permute-start.11 = (bf16[32,5120]{1,0:T(8,128)(2,1)S(1)}, bf16[32,5120]{1,0:T(8,128)(2,1)S(1)}, u32[]{:S(2)}, u32[]{:S(2)}) collective-permute-start(bf16[32,5120]{1,0:T(8,128)(2,1)S(1)} %add_convert_fusion.3), channel_id=1, source_target_pairs={{1,2},{2,1},{5,6},{6,5},{9,10},{10,9},{13,14},{14,13},{17,18},{18,... | collective-permute-start | bytes 983048 | tf_op jit(solution)/shard_map/ppermute | solution.py:238
  65.6 7.3 %collective-permute-done.7 = bf16[64,5120]{1,0:T(8,128)(2,1)S(1)} collective-permute-done((bf16[64,5120]{1,0:T(8,128)(2,1)S(1)}, bf16[64,5120]{1,0:T(8,128)(2,1)S(1)}, u32[]{:S(2)}, u32[]{:S(2)}) %collective-permute-start.7) | collective-permute-done | bytes 655392 | tf_op jit(solution)/shard_map/ppermute | solution.py:233
  72.9 3.9 %collective-permute-done.11 = bf16[32,5120]{1,0:T(8,128)(2,1)S(1)} collective-permute-done((bf16[32,5120]{1,0:T(8,128)(2,1)S(1)}, bf16[32,5120]{1,0:T(8,128)(2,1)S(1)}, u32[]{:S(2)}, u32[]{:S(2)}) %collective-permute-start.11) | collective-permute-done | bytes 327712 | tf_op jit(solution)/shard_map/ppermute | solution.py:238
  76.7 1.2 %add_convert_fusion = bf16[64,5120]{1,0:T(8,128)(2,1)} fusion(bf16[64,5120]{1,0:T(8,128)(2,1)S(1)} %collective-permute-done.9, bf16[64,5120]{1,0:T(8,128)(2,1)S(1)} %collective-permute-done.7, bf16[64,5120]{1,0:T(8,128)(2,1)S(1)} %get-tuple-element.20, bf16[32,5120]{1,0:T(8,128)(2,1)S(1)} %collective-permute-done.13, ...), kind=kLoop, calls=%fused_computation | loop fusion | flops 3604480 | bytes 3276800 | tf_op jit(solution)/shard_map/convert_element_type | solution.py:159
  (11 shorter events, 0.1 us)
Async XLA Ops:
  0.0 5.7 %copy-start.2 = (bf16[256,1024]{1,0:T(8,128)(2,1)S(1)}, bf16[256,1024]{1,0:T(8,128)(2,1)}, u32[]{:S(2)}) copy-start(bf16[256,1024]{1,0:T(8,128)(2,1)} %refs_0_.1) | copy-start | bytes 1572868
  1.8 12.2 %collective-permute-start.3 = (bf16[256,512]{1,0:T(8,128)(2,1)}, bf16[256,512]{1,0:T(8,128)(2,1)S(1)}, u32[]{:S(2)}, u32[]{:S(2)}) collective-permute-start(bf16[256,512]{1,0:T(8,128)(2,1)} %shard_map.47.refs_0_), channel_id=1, source_target_pairs={{0,24},{4,28},{8,16},{12,20},{1,25},{5,29},{9,17},{13,21},{2,26},{... | collective-permute-start | bytes 786440 | tf_op jit(solution)/shard_map/ppermute | solution.py:189
  3.1 15.4 %collective-permute-start.2 = (bf16[256,512]{1,0:T(8,128)(2,1)}, bf16[256,512]{1,0:T(8,128)(2,1)S(1)}, u32[]{:S(2)}, u32[]{:S(2)}) collective-permute-start(bf16[256,512]{1,0:T(8,128)(2,1)} %shard_map.47.refs_0_), channel_id=1, source_target_pairs={{0,16},{4,20},{8,24},{12,28},{1,17},{5,21},{9,25},{13,29},{2,18},{... | collective-permute-start | bytes 786440 | tf_op jit(solution)/shard_map/ppermute | solution.py:189
  4.4 14.1 %collective-permute-start.1 = (bf16[256,512]{1,0:T(8,128)(2,1)}, bf16[256,512]{1,0:T(8,128)(2,1)S(1)}, u32[]{:S(2)}, u32[]{:S(2)}) collective-permute-start(bf16[256,512]{1,0:T(8,128)(2,1)} %shard_map.47.refs_0_), channel_id=1, source_target_pairs={{0,8},{4,12},{16,24},{20,28},{1,9},{5,13},{17,25},{21,29},{2,10},{... | collective-permute-start | bytes 786440 | tf_op jit(solution)/shard_map/ppermute | solution.py:189
  5.7 13.3 %collective-permute-start = (bf16[256,512]{1,0:T(8,128)(2,1)}, bf16[256,512]{1,0:T(8,128)(2,1)S(1)}, u32[]{:S(2)}, u32[]{:S(2)}) collective-permute-start(bf16[256,512]{1,0:T(8,128)(2,1)} %shard_map.47.refs_0_), channel_id=1, source_target_pairs={{0,4},{4,0},{8,12},{12,8},{16,20},{20,16},{24,28},{28,24},{1,5},{5... | collective-permute-start | bytes 786440 | tf_op jit(solution)/shard_map/ppermute | solution.py:202
  5.7 4.0 %copy-start = (bf16[1024,5120]{1,0:T(8,128)(2,1)S(1)}, bf16[1024,5120]{1,0:T(8,128)(2,1)}, u32[]{:S(2)}) copy-start(bf16[1024,5120]{1,0:T(8,128)(2,1)} %refs_1_.1) | copy-start | bytes 31457284
  9.7 11.0 %copy-start.1 = (bf16[256,512]{1,0:T(8,128)(2,1)S(1)}, bf16[256,512]{1,0:T(8,128)(2,1)}, u32[]{:S(2)}) copy-start(bf16[256,512]{1,0:T(8,128)(2,1)} %shard_map.47.refs_0_) | copy-start | bytes 786436
  18.4 1.5 %collective-permute-start.4 = (bf16[256,512]{1,0:T(8,128)(2,1)S(1)}, bf16[256,512]{1,0:T(8,128)(2,1)S(1)}, u32[]{:S(2)}, u32[]{:S(2)}) collective-permute-start(bf16[256,512]{1,0:T(8,128)(2,1)S(1)} %collective-permute-done.1.refs_2_), channel_id=1, source_target_pairs={{0,4},{4,0},{8,12},{12,8},{16,20},{20,16},{24,28},{28,24},{1,5},{5... | collective-permute-start | bytes 786440 | tf_op jit(solution)/shard_map/ppermute | solution.py:202
  18.4 1.9 %collective-permute-start.5 = (bf16[256,512]{1,0:T(8,128)(2,1)S(1)}, bf16[256,512]{1,0:T(8,128)(2,1)S(1)}, u32[]{:S(2)}, u32[]{:S(2)}) collective-permute-start(bf16[256,512]{1,0:T(8,128)(2,1)S(1)} %collective-permute-done.2.refs_4_), channel_id=1, source_target_pairs={{0,4},{4,0},{8,12},{12,8},{16,20},{20,16},{24,28},{28,24},{1,5},{5... | collective-permute-start | bytes 786440 | tf_op jit(solution)/shard_map/ppermute | solution.py:202
  18.9 1.8 %collective-permute-start.6 = (bf16[256,512]{1,0:T(8,128)(2,1)S(1)}, bf16[256,512]{1,0:T(8,128)(2,1)S(1)}, u32[]{:S(2)}, u32[]{:S(2)}) collective-permute-start(bf16[256,512]{1,0:T(8,128)(2,1)S(1)} %collective-permute-done.3.refs_6_), channel_id=1, source_target_pairs={{0,4},{4,0},{8,12},{12,8},{16,20},{20,16},{24,28},{28,24},{1,5},{5... | collective-permute-start | bytes 786440 | tf_op jit(solution)/shard_map/ppermute | solution.py:202
  26.1 19.5 %collective-permute-start.8 = (bf16[64,5120]{1,0:T(8,128)(2,1)S(1)}, bf16[64,5120]{1,0:T(8,128)(2,1)S(1)}, u32[]{:S(2)}, u32[]{:S(2)}) collective-permute-start(bf16[64,5120]{1,0:T(8,128)(2,1)S(1)} %shard_map.49), channel_id=1, source_target_pairs={{0,1},{3,2},{4,5},{7,6},{8,9},{11,10},{12,13},{15,14},{16,17},{19,... | collective-permute-start | bytes 1966088 | tf_op jit(solution)/shard_map/ppermute | solution.py:227
  36.7 15.9 %collective-permute-start.10 = (bf16[32,5120]{1,0:T(8,128)(2,1)S(1)}, bf16[32,5120]{1,0:T(8,128)(2,1)S(1)}, u32[]{:S(2)}, u32[]{:S(2)}) collective-permute-start(bf16[32,5120]{1,0:T(8,128)(2,1)S(1)} %get-tuple-element.25), channel_id=1, source_target_pairs={{0,1},{3,2},{4,5},{7,6},{8,9},{11,10},{12,13},{15,14},{16,17},{19,... | collective-permute-start | bytes 983048 | tf_op jit(solution)/shard_map/ppermute | solution.py:232
  38.0 21.6 %collective-permute-start.12 = (bf16[32,5120]{1,0:T(8,128)(2,1)S(1)}, bf16[32,5120]{1,0:T(8,128)(2,1)S(1)}, u32[]{:S(2)}, u32[]{:S(2)}) collective-permute-start(bf16[32,5120]{1,0:T(8,128)(2,1)S(1)} %get-tuple-element.26), channel_id=1, source_target_pairs={{0,1},{3,2},{4,5},{7,6},{8,9},{11,10},{12,13},{15,14},{16,17},{19,... | collective-permute-start | bytes 983048 | tf_op jit(solution)/shard_map/ppermute | solution.py:232
  39.3 33.6 %collective-permute-start.7 = (bf16[64,5120]{1,0:T(8,128)(2,1)S(1)}, bf16[64,5120]{1,0:T(8,128)(2,1)S(1)}, u32[]{:S(2)}, u32[]{:S(2)}) collective-permute-start(bf16[64,5120]{1,0:T(8,128)(2,1)S(1)} %get-tuple-element.21), channel_id=1, source_target_pairs={{0,1},{1,0},{2,3},{3,2},{4,5},{5,4},{6,7},{7,6},{8,9},{9,8},{10,11... | collective-permute-start | bytes 1966088 | tf_op jit(solution)/shard_map/ppermute | solution.py:233
  45.7 31.0 %collective-permute-start.9 = (bf16[64,5120]{1,0:T(8,128)(2,1)S(1)}, bf16[64,5120]{1,0:T(8,128)(2,1)S(1)}, u32[]{:S(2)}, u32[]{:S(2)}) collective-permute-start(bf16[64,5120]{1,0:T(8,128)(2,1)S(1)} %add_convert_fusion.1), channel_id=1, source_target_pairs={{1,3},{2,0},{5,7},{6,4},{9,11},{10,8},{13,15},{14,12},{17,19},{18,... | collective-permute-start | bytes 1966088 | tf_op jit(solution)/shard_map/ppermute | solution.py:235
  59.7 13.2 %collective-permute-start.13 = (bf16[32,5120]{1,0:T(8,128)(2,1)S(1)}, bf16[32,5120]{1,0:T(8,128)(2,1)S(1)}, u32[]{:S(2)}, u32[]{:S(2)}) collective-permute-start(bf16[32,5120]{1,0:T(8,128)(2,1)S(1)} %add_convert_fusion.2), channel_id=1, source_target_pairs={{1,2},{2,1},{5,6},{6,5},{9,10},{10,9},{13,14},{14,13},{17,18},{18,... | collective-permute-start | bytes 983048 | tf_op jit(solution)/shard_map/ppermute | solution.py:238
  62.1 14.7 %collective-permute-start.11 = (bf16[32,5120]{1,0:T(8,128)(2,1)S(1)}, bf16[32,5120]{1,0:T(8,128)(2,1)S(1)}, u32[]{:S(2)}, u32[]{:S(2)}) collective-permute-start(bf16[32,5120]{1,0:T(8,128)(2,1)S(1)} %add_convert_fusion.3), channel_id=1, source_target_pairs={{1,2},{2,1},{5,6},{6,5},{9,10},{10,9},{13,14},{14,13},{17,18},{18,... | collective-permute-start | bytes 983048 | tf_op jit(solution)/shard_map/ppermute | solution.py:238

commit v3 on v2

--- a/solution.py
+++ b/solution.py
@@ -15,6 +15,7 @@
 EXPONENT = HEAD_DIMENSION ** (-0.5) * math.log2(math.e)
 NEGATIVE = -1e30
 TILE = 512
+GROUP = 6
 
 
 def dot(a, b):
@@ -33,12 +34,12 @@
     return jnp.broadcast_to(column, (column.shape[0], HEAD_DIMENSION))
 
 
-def keys_of(first, second, g):
-    return jnp.concatenate([first[:, head(g)], second[:, head(g)]], axis=0)
-
-
-def values_of(first, second, g, kv_here):
-    values = keys_of(first, second, kv_here + g)
+def keys_of(blocks, g):
+    return jnp.concatenate([block[:, head(g)] for block in blocks], axis=0)
+
+
+def values_of(blocks, g, kv_here):
+    values = keys_of(blocks, kv_here + g)
     return jnp.concatenate([values, jnp.ones_like(values)], axis=1)
 
 
@@ -75,12 +76,17 @@
         copy.wait()
 
 
-def layer_kernel(q_ref, *refs, heads, per_kv, chips, order):
+def layer_kernel(q_ref, *refs, heads, per_kv, chips, order, hops, first, last):
     chunks = len(order)
-    kv_ref, refs = refs[: 2 * chips], refs[2 * chips :]
-    w_ref, outs, refs = refs[0], refs[1 : 1 + chunks], refs[1 + chunks :]
-    acc_ref, top_ref, att_ref = refs
-    rows = outs[0].shape[0]
+    count = 2 * first + len(hops)
+    kv_ref, refs = refs[:count], refs[count:]
+    if not first:
+        acc_in, top_in, refs = refs[0], refs[1], refs[2:]
+    if last:
+        w_ref, outs, (acc_ref, top_ref, att_ref) = refs[0], refs[1 : 1 + chunks], refs[1 + chunks :]
+    else:
+        acc_ref, top_ref = refs
+    rows = acc_ref.shape[2] // per_kv
     tok = kv_ref[0].shape[0]
     kv_here = heads // per_kv
     place = lax.rem(lax.axis_index("seq"), 2 * chips)
@@ -97,32 +103,44 @@
                 step(i, g, jnp.concatenate([q_ref[there[i], head(h)] for h in mine], axis=0))
 
     def own(i, g, query):
-        score = dot_nt(query, keys_of(kv_ref[0], kv_ref[1], g))
+        score = dot_nt(query, keys_of(kv_ref[:2], g))
         row = lax.broadcasted_iota(jnp.int32, score.shape, 0) % rows + starts[i]
         col = lax.broadcasted_iota(jnp.int32, score.shape, 1)
         score = jnp.where(col <= jnp.where(col < tok, row, core * 2 * tok), score, NEGATIVE)
         top = jnp.max(score, axis=1, keepdims=True)
         weight = jnp.exp2((score - top) * EXPONENT).astype(jnp.bfloat16)
-        acc_ref[i, g] = dot(weight, values_of(kv_ref[0], kv_ref[1], g, kv_here))
+        acc_ref[i, g] = dot(weight, values_of(kv_ref[:2], g, kv_here))
         top_ref[i, g] = spread(top)
 
-    def others(i, g, query, pair=None):
+    def others(i, g, query, seen=None):
         acc_ref[i, g], top_ref[i, g] = folded(
-            query,
-            keys_of(*pair, g),
-            values_of(*pair, g, kv_here),
-            acc_ref[i, g],
-            top_ref[i, g],
+            query, keys_of(seen, g), values_of(seen, g, kv_here), acc_ref[i, g], top_ref[i, g]
         )
 
-    for d in range(chips):
-        if d == 0:
-            every(own)
-        else:
-            pair = (kv_ref[2 * d], kv_ref[2 * d + 1])
-            pl.when((chip ^ d) < chip)(
-                functools.partial(every, functools.partial(others, pair=pair))
-            )
+    if first:
+        every(own)
+    else:
+        acc_ref[...] = acc_in[...]
+        top_ref[...] = top_in[...]
+    blocks = kv_ref[2 * first :]
+    bits = sorted({d.bit_length() - 1 for d in hops})
+    some = {bit: [x for d, x in zip(hops, blocks) if d.bit_length() - 1 == bit] for bit in bits}
+    seen = {bit: (chip >> bit) & 1 == 1 for bit in bits}
+
+    def add(case, group):
+        pl.when(case)(functools.partial(every, functools.partial(others, seen=group)))
+
+    if len(hops) <= GROUP and len(bits) == 2:
+        low, high = bits
+        add(seen[low] & seen[high], some[high] + some[low])
+        add(seen[low] & ~seen[high], some[low])
+        add(~seen[low] & seen[high], some[high])
+    else:
+        for bit in bits:
+            for at in range(0, len(some[bit]), GROUP):
+                add(seen[bit], some[bit][at : at + GROUP])
+    if not last:
+        return
     for i in range(chunks):
         for h in range(heads):
             g, j = h // per_kv, h % per_kv
@@ -197,46 +215,70 @@
         place=pl.ANY,
     )
     blocks[1:] = lax.optimization_barrier((*blocks[1:], q_here, w_here))[: chips - 1]
-    both = []
-    for block in blocks:
-        both += [block, lax.ppermute(block, "seq", swap)]
-
-    def layer(order, rows):
+    swapped = [lax.ppermute(block, "seq", swap) for block in blocks]
+    hops = list(range(1, chips))
+
+    def layer(order, rows, seen, state=None, first=True, last=True):
         chunks = len(order)
+        running = [(chunks, kv_here, per_kv * rows, 2 * hd), (chunks, kv_here, per_kv * rows, hd)]
+        own_blocks = [own, swapped[0]] if first else []
+        args = [*own_blocks, *[block for _, block in seen], *(state or []), *([w_here] * last)]
         return call(
-            functools.partial(layer_kernel, heads=heads, per_kv=per_kv, chips=chips, order=order),
-            [jax.ShapeDtypeStruct((rows, width), jnp.bfloat16)] * chunks,
+            functools.partial(
+                layer_kernel,
+                heads=heads,
+                per_kv=per_kv,
+                chips=chips,
+                order=order,
+                hops=[d for d, _ in seen],
+                first=first,
+                last=last,
+            ),
+            [jax.ShapeDtypeStruct((rows, width), jnp.bfloat16)] * chunks
+            if last
+            else [jax.ShapeDtypeStruct(shape, jnp.float32) for shape in running],
             q_here,
-            *both,
-            w_here,
-            scratch=[
-                pltpu.VMEM((chunks, kv_here, per_kv * rows, 2 * hd), jnp.float32),
-                pltpu.VMEM((chunks, kv_here, per_kv * rows, hd), jnp.float32),
-                pltpu.VMEM((rows * chunks, heads * hd), jnp.bfloat16),
-            ],
+            *args,
+            scratch=[pltpu.VMEM(shape, jnp.float32) for shape in running]
+            + [pltpu.VMEM((rows * chunks, heads * hd), jnp.bfloat16)]
+            if last
+            else [],
             limit=24,
         )
 
+    got = list(zip(hops, blocks[1:]))
+    theirs = list(zip(hops, swapped[1:]))
     if tp_devs != 4:
-        (part,) = layer([lambda at: 0], tok)
+        (part,) = layer([lambda at: 0], tok, got + theirs)
         return lax.psum_scatter(part, "tp", scatter_dimension=0, tiled=True)
 
     rows = tok // 4
-    (far,) = layer([lambda at: jnp.where(at < 2, 3, 0)], rows)
+    far_rows = [lambda at: jnp.where(at < 2, 3, 0)]
+    state = layer(far_rows, rows, got, last=False)
+    (far,) = layer(far_rows, rows, theirs, state, first=False)
     inward, sides = [(0, 1), (3, 2)], [(0, 1), (1, 0), (2, 3), (3, 2)]
     got_far = lax.ppermute(far, "tp", inward)
     near, side, mine = layer(
-        [lambda at: jnp.where(at < 2, 2, 1), lambda at: at ^ 1, lambda at: at], rows
-    )
-    halves = [near[: rows // 2], near[rows // 2 :]]
-    got_near = [lax.ppermute(x, "tp", inward) for x in halves]
+        [lambda at: jnp.where(at < 2, 2, 1), lambda at: at ^ 1, lambda at: at], rows, got + theirs
+    )
+    half = rows // 2
+    early, late = near[:half], near[half:]
+    outward = [(1, 2), (2, 1)]
+    got_direct = lax.ppermute(early, "tp", [(0, 2), (3, 1)])
+    got_late = lax.ppermute(late, "tp", inward)
     got_side = lax.ppermute(side, "tp", sides)
-    last = added(got_far, far)
-    across = [lax.ppermute(last, "tp", [(1, 3), (2, 0)])]
-    for got, x in zip(got_near, halves):
-        last = added(after(got, last), x)
-        across.append(lax.ppermute(last, "tp", [(1, 2), (2, 1)]))
-    return added(mine, got_side, across[0], jnp.concatenate(across[1:], axis=0))
+    got_early = lax.ppermute(early, "tp", outward)
+    total_far = added(got_far, far)
+    across_far = lax.ppermute(total_far, "tp", [(1, 3), (2, 0)])
+    got_late = after(got_late, got_direct, got_early, total_far)
+    across_late = lax.ppermute(added(got_late, late), "tp", outward)
+    return jnp.concatenate(
+        [
+            added(mine[:half], got_side[:half], across_far[:half], got_direct, got_early),
+            added(mine[half:], got_side[half:], across_far[half:], across_late),
+        ],
+        axis=0,
+    )
 
 
 def solution(mesh):

time: 78.2 us -> 74.1 us (0.948)
  Pallas kernels: 17.1 us -> 14.6 us
  waiting for transfers between devices: 36.8 us -> 35.4 us
    ppermute x9, waiting for transfers between devices: 18.1 us -> 14.1 us  [the longest x1 12.6 us: body(): got_late = lax.ppermute(late, 'tp', inward)]
    ppermute x1, waiting for transfers between devices: 7.3 us -> 11.2 us  [body(): got_side = lax.ppermute(side, 'tp', sides)]
    pallas_call x4 -> x5, Pallas kernels: 17.1 us -> 14.6 us  [call(): pl.pallas_call(kernel, out_shape=out_shape, in_specs=[pl.BlockSpec(memory...]
    ppermute x1, waiting for transfers between devices: 3.52 us -> 2.1 us  [body(): got_far = lax.ppermute(far, 'tp', inward)]
    ppermute x9, starting transfers between devices: 10.4 us -> 9.27 us  [the longest x1 2.36 us: body(): got_early = lax.ppermute(early, 'tp', outward)]
    ppermute x1, starting transfers between devices: 2.78 us -> 3.76 us  [body(): got_side = lax.ppermute(side, 'tp', sides)]
    concatenate x0 -> x1, other arithmetic: none -> 0.88 us  [body(): jnp.concatenate([added(mine[:half], got_side[:half], across_far[:half], g...]
    convert_element_type x4 -> x3, other arithmetic: 1.47 us -> 0.6 us  [added(): return total.astype(terms[0].dtype)]
  transfers between devices with their start and end apart: 14 -> 14, of which waited for: 10 -> 6; matrix products, arithmetic and copies ran while one was open for 0% -> 0% of each run, Pallas kernels for 13% -> 13%
where the time goes in v3:
time: 74.1 us; the launch traced here: 73.8 us
  waiting for transfers between devices  35.4 us (48%)
  starting transfers between devices  18.2 us (25%)
  Pallas kernels  14.6 us (20%)
  local copies, waits for them, and re-layouts  4.03 us (5%)
  other arithmetic  1.48 us (2%)
    pallas_call x5, Pallas kernels, call(): pl.pallas_call(kernel, out_shape=out_shape, in_specs=[pl.BlockSpec(memory...  14.6 us
    ppermute x1, waiting for transfers between devices, body(): got_late = lax.ppermute(late, 'tp', inward)  12.6 us
    ppermute x1, waiting for transfers between devices, body(): got_side = lax.ppermute(side, 'tp', sides)  11.2 us
    ppermute x3, waiting for transfers between devices, body(): blocks.append(lax.ppermute(own, 'seq', pairs))  7.94 us
    unnamed x6, local copies, waits for them, and re-layouts  3.98 us
    ppermute x3, starting transfers between devices, body(): blocks.append(lax.ppermute(own, 'seq', pairs))  3.88 us
    ppermute x1, starting transfers between devices, body(): got_side = lax.ppermute(side, 'tp', sides)  3.76 us
    ppermute x1, starting transfers between devices, body(): got_early = lax.ppermute(early, 'tp', outward)  2.36 us
  transfers between devices with their start and end apart: 14, of which 6 were waited for; matrix products, arithmetic and copies ran while one was open for 0% of the time, Pallas kernels for 13%

profile of v3, /device:TPU:22, one launch (start us, length us, event | category | flops | bytes accessed | tf_op | source)
XLA Modules:
  0.0 73.8 jit_solution(12854962845689191446)
XLA Ops:
  0.0 1.7 %shard_map.47.refs_0_ = bf16[256,512]{1,0:T(8,128)(2,1)} custom-call(bf16[256,1024]{1,0:T(8,128)(2,1)} %keys.1, bf16[256,1024]{1,0:T(8,128)(2,1)} %values.1), custom_call_target="tpu_custom_call" | custom-call | tf_op jit(solution)/shard_map/pallas_call | solution.py:159
  1.8 1.3 %collective-permute-start.3 = (bf16[256,512]{1,0:T(8,128)(2,1)}, bf16[256,512]{1,0:T(8,128)(2,1)S(1)}, u32[]{:S(2)}, u32[]{:S(2)}) collective-permute-start(bf16[256,512]{1,0:T(8,128)(2,1)} %shard_map.47.refs_0_), channel_id=1, source_target_pairs={{0,24},{4,28},{8,16},{12,20},{1,25},{5,29},{9,17},{13,21},{2,26},{... | collective-permute-start | bytes 786440 | tf_op jit(solution)/shard_map/ppermute | solution.py:207
  3.1 1.3 %collective-permute-start.2 = (bf16[256,512]{1,0:T(8,128)(2,1)}, bf16[256,512]{1,0:T(8,128)(2,1)S(1)}, u32[]{:S(2)}, u32[]{:S(2)}) collective-permute-start(bf16[256,512]{1,0:T(8,128)(2,1)} %shard_map.47.refs_0_), channel_id=1, source_target_pairs={{0,16},{4,20},{8,24},{12,28},{1,17},{5,21},{9,25},{13,29},{2,18},{... | collective-permute-start | bytes 786440 | tf_op jit(solution)/shard_map/ppermute | solution.py:207
  4.4 1.3 %collective-permute-start.1 = (bf16[256,512]{1,0:T(8,128)(2,1)}, bf16[256,512]{1,0:T(8,128)(2,1)S(1)}, u32[]{:S(2)}, u32[]{:S(2)}) collective-permute-start(bf16[256,512]{1,0:T(8,128)(2,1)} %shard_map.47.refs_0_), channel_id=1, source_target_pairs={{0,8},{4,12},{16,24},{20,28},{1,9},{5,13},{17,25},{21,29},{2,10},{... | collective-permute-start | bytes 786440 | tf_op jit(solution)/shard_map/ppermute | solution.py:207
  5.7 0.1 collective-permute-start
  5.7 0.0 copy-start
  5.8 4.0 %copy-done = bf16[1024,5120]{1,0:T(8,128)(2,1)S(1)} copy-done((bf16[1024,5120]{1,0:T(8,128)(2,1)S(1)}, bf16[1024,5120]{1,0:T(8,128)(2,1)}, u32[]{:S(2)}) %copy-start) | copy-done | bytes 10485784
  9.7 0.8 %shard_map.46 = (bf16[256,1024]{1,0:T(8,128)(2,1)S(1)}, bf16[1024,5120]{1,0:T(8,128)(2,1)S(1)}) custom-call(bf16[256,1024]{1,0:T(8,128)(2,1)S(1)} %copy-done.2, bf16[1024,5120]{1,0:T(8,128)(2,1)S(1)} %copy-done), custom_call_target="tpu_custom_call" | custom-call | tf_op jit(solution)/shard_map/pallas_call | solution.py:159
  10.5 3.5 %collective-permute-done.3.refs_4_ = bf16[256,512]{1,0:T(8,128)(2,1)S(1)} collective-permute-done((bf16[256,512]{1,0:T(8,128)(2,1)}, bf16[256,512]{1,0:T(8,128)(2,1)S(1)}, u32[]{:S(2)}, u32[]{:S(2)}) %collective-permute-start.3) | collective-permute-done | bytes 262176 | tf_op jit(solution)/shard_map/ppermute | solution.py:207
  14.0 4.4 %collective-permute-done.2.refs_3_ = bf16[256,512]{1,0:T(8,128)(2,1)S(1)} collective-permute-done((bf16[256,512]{1,0:T(8,128)(2,1)}, bf16[256,512]{1,0:T(8,128)(2,1)S(1)}, u32[]{:S(2)}, u32[]{:S(2)}) %collective-permute-start.2) | collective-permute-done | bytes 262176 | tf_op jit(solution)/shard_map/ppermute | solution.py:207
  18.4 0.0 collective-permute-done.1.refs_2_
  18.4 0.0 collective-permute-start.4
  18.4 0.5 collective-permute-start.5
  18.9 0.0 collective-permute-start.6
  19.0 1.8 %shard_map.49 = (f32[1,2,256,256]{3,2,1,0:T(8,128)S(1)}, f32[1,2,256,128]{3,2,1,0:T(8,128)S(1)}) custom-call(bf16[256,1024]{1,0:T(8,128)(2,1)S(1)} %get-tuple-element.16.q_ref, bf16[256,512]{1,0:T(8,128)(2,1)S(1)} %copy-done.1, bf16[256,512]{1,0:T(8,128)(2,1)S(1)} %collective-permute-done.refs_1_, bf16[256,512]{1,0:T(8,128)(2,1)S(1)} %collective-permute-done.1.refs_2_, ...), custom_call_target="tpu_custom_call" | custom-call | tf_op jit(solution)/shard_map/pallas_call | solution.py:159
  20.8 3.1 %shard_map.50 = bf16[64,5120]{1,0:T(8,128)(2,1)S(1)} custom-call(bf16[256,1024]{1,0:T(8,128)(2,1)S(1)} %get-tuple-element.16.q_ref, bf16[256,512]{1,0:T(8,128)(2,1)S(1)} %collective-permute-done.4.refs_5_.refs_0_, bf16[256,512]{1,0:T(8,128)(2,1)S(1)} %collective-permute-done.5.refs_6_.refs_1_, bf16[256,512]{1,0:T(8,128)(2,1)S(1)} %collective-permute-done.6.refs_7_.refs_2_, ...), custom_call_target="tpu_custom_call" | custom-call | tf_op jit(solution)/shard_map/pallas_call | solution.py:159
  23.8 1.3 %collective-permute-start.8 = (bf16[64,5120]{1,0:T(8,128)(2,1)S(1)}, bf16[64,5120]{1,0:T(8,128)(2,1)S(1)}, u32[]{:S(2)}, u32[]{:S(2)}) collective-permute-start(bf16[64,5120]{1,0:T(8,128)(2,1)S(1)} %shard_map.50), channel_id=1, source_target_pairs={{0,1},{3,2},{4,5},{7,6},{8,9},{11,10},{12,13},{15,14},{16,17},{19,... | collective-permute-start | bytes 1966088 | tf_op jit(solution)/shard_map/ppermute | solution.py:260
  25.1 7.2 %shard_map.48 = (bf16[64,5120]{1,0:T(8,128)(2,1)S(1)}, bf16[64,5120]{1,0:T(8,128)(2,1)S(1)}, bf16[64,5120]{1,0:T(8,128)(2,1)S(1)}) custom-call(bf16[256,1024]{1,0:T(8,128)(2,1)S(1)} %get-tuple-element.16.q_ref, bf16[256,512]{1,0:T(8,128)(2,1)S(1)} %copy-done.1, bf16[256,512]{1,0:T(8,128)(2,1)S(1)} %collective-permute-done.refs_1_, ...), custom_call_target="tpu_custom_call" | custom-call | tf_op jit(solution)/shard_map/pallas_call | solution.py:159
  32.4 2.4 %collective-permute-start.11 = (bf16[32,5120]{1,0:T(8,128)(2,1)S(1)}, bf16[32,5120]{1,0:T(8,128)(2,1)S(1)}, u32[]{:S(2)}, u32[]{:S(2)}) collective-permute-start(bf16[32,5120]{1,0:T(8,128)(2,1)S(1)} %get-tuple-element.29), channel_id=1, source_target_pairs={{1,2},{2,1},{5,6},{6,5},{9,10},{10,9},{13,14},{14,13},{17,18},{18,... | collective-permute-start | bytes 983048 | tf_op jit(solution)/shard_map/ppermute | solution.py:270
  34.8 1.3 %collective-permute-start.10 = (bf16[32,5120]{1,0:T(8,128)(2,1)S(1)}, bf16[32,5120]{1,0:T(8,128)(2,1)S(1)}, u32[]{:S(2)}, u32[]{:S(2)}) collective-permute-start(bf16[32,5120]{1,0:T(8,128)(2,1)S(1)} %get-tuple-element.29), channel_id=1, source_target_pairs={{0,2},{3,1},{4,6},{7,5},{8,10},{11,9},{12,14},{15,13},{16,18},{19,... | collective-permute-start | bytes 983048 | tf_op jit(solution)/shard_map/ppermute | solution.py:267
  36.1 1.3 %collective-permute-start.12 = (bf16[32,5120]{1,0:T(8,128)(2,1)S(1)}, bf16[32,5120]{1,0:T(8,128)(2,1)S(1)}, u32[]{:S(2)}, u32[]{:S(2)}) collective-permute-start(bf16[32,5120]{1,0:T(8,128)(2,1)S(1)} %get-tuple-element.30), channel_id=1, source_target_pairs={{0,1},{3,2},{4,5},{7,6},{8,9},{11,10},{12,13},{15,14},{16,17},{19,... | collective-permute-start | bytes 983048 | tf_op jit(solution)/shard_map/ppermute | solution.py:268
  37.4 3.8 %collective-permute-start.7 = (bf16[64,5120]{1,0:T(8,128)(2,1)S(1)}, bf16[64,5120]{1,0:T(8,128)(2,1)S(1)}, u32[]{:S(2)}, u32[]{:S(2)}) collective-permute-start(bf16[64,5120]{1,0:T(8,128)(2,1)S(1)} %get-tuple-element.22), channel_id=1, source_target_pairs={{0,1},{1,0},{2,3},{3,2},{4,5},{5,4},{6,7},{7,6},{8,9},{9,8},{10,11... | collective-permute-start | bytes 1966088 | tf_op jit(solution)/shard_map/ppermute | solution.py:269
  41.2 2.1 %collective-permute-done.8 = bf16[64,5120]{1,0:T(8,128)(2,1)S(1)} collective-permute-done((bf16[64,5120]{1,0:T(8,128)(2,1)S(1)}, bf16[64,5120]{1,0:T(8,128)(2,1)S(1)}, u32[]{:S(2)}, u32[]{:S(2)}) %collective-permute-start.8) | collective-permute-done | bytes 655392 | tf_op jit(solution)/shard_map/ppermute | solution.py:260
  43.3 0.2 add_convert_fusion
  43.4 1.4 %collective-permute-start.9 = (bf16[64,5120]{1,0:T(8,128)(2,1)S(1)}, bf16[64,5120]{1,0:T(8,128)(2,1)S(1)}, u32[]{:S(2)}, u32[]{:S(2)}) collective-permute-start(bf16[64,5120]{1,0:T(8,128)(2,1)S(1)} %add_convert_fusion), channel_id=1, source_target_pairs={{1,3},{2,0},{5,7},{6,4},{9,11},{10,8},{13,15},{14,12},{17,19},{18,... | collective-permute-start | bytes 1966088 | tf_op jit(solution)/shard_map/ppermute | solution.py:272
  44.8 12.6 %collective-permute-done.12 = bf16[32,5120]{1,0:T(8,128)(2,1)S(1)} collective-permute-done((bf16[32,5120]{1,0:T(8,128)(2,1)S(1)}, bf16[32,5120]{1,0:T(8,128)(2,1)S(1)}, u32[]{:S(2)}, u32[]{:S(2)}) %collective-permute-start.12) | collective-permute-done | bytes 327712 | tf_op jit(solution)/shard_map/ppermute | solution.py:268
  57.4 0.1 add_convert_fusion.2
  57.5 2.4 %collective-permute-start.13 = (bf16[32,5120]{1,0:T(8,128)(2,1)S(1)}, bf16[32,5120]{1,0:T(8,128)(2,1)S(1)}, u32[]{:S(2)}, u32[]{:S(2)}) collective-permute-start(bf16[32,5120]{1,0:T(8,128)(2,1)S(1)} %add_convert_fusion.2), channel_id=1, source_target_pairs={{1,2},{2,1},{5,6},{6,5},{9,10},{10,9},{13,14},{14,13},{17,18},{18,... | collective-permute-start | bytes 983048 | tf_op jit(solution)/shard_map/ppermute | solution.py:274
  59.8 11.2 %collective-permute-done.7 = bf16[64,5120]{1,0:T(8,128)(2,1)S(1)} collective-permute-done((bf16[64,5120]{1,0:T(8,128)(2,1)S(1)}, bf16[64,5120]{1,0:T(8,128)(2,1)S(1)}, u32[]{:S(2)}, u32[]{:S(2)}) %collective-permute-start.7) | collective-permute-done | bytes 655392 | tf_op jit(solution)/shard_map/ppermute | solution.py:269
  71.0 1.6 %collective-permute-done.13 = bf16[32,5120]{1,0:T(8,128)(2,1)S(1)} collective-permute-done((bf16[32,5120]{1,0:T(8,128)(2,1)S(1)}, bf16[32,5120]{1,0:T(8,128)(2,1)S(1)}, u32[]{:S(2)}, u32[]{:S(2)}) %collective-permute-start.13) | collective-permute-done | bytes 327712 | tf_op jit(solution)/shard_map/ppermute | solution.py:274
  72.6 0.4 add_convert_fusion.3
  73.0 0.9 %pad_maximum_fusion = bf16[64,5120]{1,0:T(8,128)(2,1)} fusion(bf16[32,5120]{1,0:T(8,128)(2,1)S(1)} %get-tuple-element.28, bf16[32,5120]{1,0:T(8,128)(2,1)S(1)} %get-tuple-element.27), kind=kLoop, calls=%fused_computation.1 | loop fusion | flops 1310720 | bytes 1310720 | tf_op jit(solution)/shard_map/concatenate | solution.py:275
  (12 shorter events, 0.1 us)
Async XLA Ops:
  0.0 5.7 %copy-start.2 = (bf16[256,1024]{1,0:T(8,128)(2,1)S(1)}, bf16[256,1024]{1,0:T(8,128)(2,1)}, u32[]{:S(2)}) copy-start(bf16[256,1024]{1,0:T(8,128)(2,1)} %refs_0_.1) | copy-start | bytes 1572868
  1.8 12.2 %collective-permute-start.3 = (bf16[256,512]{1,0:T(8,128)(2,1)}, bf16[256,512]{1,0:T(8,128)(2,1)S(1)}, u32[]{:S(2)}, u32[]{:S(2)}) collective-permute-start(bf16[256,512]{1,0:T(8,128)(2,1)} %shard_map.47.refs_0_), channel_id=1, source_target_pairs={{0,24},{4,28},{8,16},{12,20},{1,25},{5,29},{9,17},{13,21},{2,26},{... | collective-permute-start | bytes 786440 | tf_op jit(solution)/shard_map/ppermute | solution.py:207
  3.1 15.4 %collective-permute-start.2 = (bf16[256,512]{1,0:T(8,128)(2,1)}, bf16[256,512]{1,0:T(8,128)(2,1)S(1)}, u32[]{:S(2)}, u32[]{:S(2)}) collective-permute-start(bf16[256,512]{1,0:T(8,128)(2,1)} %shard_map.47.refs_0_), channel_id=1, source_target_pairs={{0,16},{4,20},{8,24},{12,28},{1,17},{5,21},{9,25},{13,29},{2,18},{... | collective-permute-start | bytes 786440 | tf_op jit(solution)/shard_map/ppermute | solution.py:207
  4.4 14.1 %collective-permute-start.1 = (bf16[256,512]{1,0:T(8,128)(2,1)}, bf16[256,512]{1,0:T(8,128)(2,1)S(1)}, u32[]{:S(2)}, u32[]{:S(2)}) collective-permute-start(bf16[256,512]{1,0:T(8,128)(2,1)} %shard_map.47.refs_0_), channel_id=1, source_target_pairs={{0,8},{4,12},{16,24},{20,28},{1,9},{5,13},{17,25},{21,29},{2,10},{... | collective-permute-start | bytes 786440 | tf_op jit(solution)/shard_map/ppermute | solution.py:207
  5.7 13.3 %collective-permute-start = (bf16[256,512]{1,0:T(8,128)(2,1)}, bf16[256,512]{1,0:T(8,128)(2,1)S(1)}, u32[]{:S(2)}, u32[]{:S(2)}) collective-permute-start(bf16[256,512]{1,0:T(8,128)(2,1)} %shard_map.47.refs_0_), channel_id=1, source_target_pairs={{0,4},{4,0},{8,12},{12,8},{16,20},{20,16},{24,28},{28,24},{1,5},{5... | collective-permute-start | bytes 786440 | tf_op jit(solution)/shard_map/ppermute | solution.py:218
  5.7 4.0 %copy-start = (bf16[1024,5120]{1,0:T(8,128)(2,1)S(1)}, bf16[1024,5120]{1,0:T(8,128)(2,1)}, u32[]{:S(2)}) copy-start(bf16[1024,5120]{1,0:T(8,128)(2,1)} %refs_1_.1) | copy-start | bytes 31457284
  9.7 9.2 %copy-start.1 = (bf16[256,512]{1,0:T(8,128)(2,1)S(1)}, bf16[256,512]{1,0:T(8,128)(2,1)}, u32[]{:S(2)}) copy-start(bf16[256,512]{1,0:T(8,128)(2,1)} %shard_map.47.refs_0_) | copy-start | bytes 786436
  18.4 2.3 %collective-permute-start.4 = (bf16[256,512]{1,0:T(8,128)(2,1)S(1)}, bf16[256,512]{1,0:T(8,128)(2,1)S(1)}, u32[]{:S(2)}, u32[]{:S(2)}) collective-permute-start(bf16[256,512]{1,0:T(8,128)(2,1)S(1)} %collective-permute-done.1.refs_2_), channel_id=1, source_target_pairs={{0,4},{4,0},{8,12},{12,8},{16,20},{20,16},{24,28},{28,24},{1,5},{5... | collective-permute-start | bytes 786440 | tf_op jit(solution)/shard_map/ppermute | solution.py:218
  18.4 2.3 %collective-permute-start.5 = (bf16[256,512]{1,0:T(8,128)(2,1)S(1)}, bf16[256,512]{1,0:T(8,128)(2,1)S(1)}, u32[]{:S(2)}, u32[]{:S(2)}) collective-permute-start(bf16[256,512]{1,0:T(8,128)(2,1)S(1)} %collective-permute-done.2.refs_3_), channel_id=1, source_target_pairs={{0,4},{4,0},{8,12},{12,8},{16,20},{20,16},{24,28},{28,24},{1,5},{5... | collective-permute-start | bytes 786440 | tf_op jit(solution)/shard_map/ppermute | solution.py:218
  18.9 1.8 %collective-permute-start.6 = (bf16[256,512]{1,0:T(8,128)(2,1)S(1)}, bf16[256,512]{1,0:T(8,128)(2,1)S(1)}, u32[]{:S(2)}, u32[]{:S(2)}) collective-permute-start(bf16[256,512]{1,0:T(8,128)(2,1)S(1)} %collective-permute-done.3.refs_4_), channel_id=1, source_target_pairs={{0,4},{4,0},{8,12},{12,8},{16,20},{20,16},{24,28},{28,24},{1,5},{5... | collective-permute-start | bytes 786440 | tf_op jit(solution)/shard_map/ppermute | solution.py:218
  23.8 19.4 %collective-permute-start.8 = (bf16[64,5120]{1,0:T(8,128)(2,1)S(1)}, bf16[64,5120]{1,0:T(8,128)(2,1)S(1)}, u32[]{:S(2)}, u32[]{:S(2)}) collective-permute-start(bf16[64,5120]{1,0:T(8,128)(2,1)S(1)} %shard_map.50), channel_id=1, source_target_pairs={{0,1},{3,2},{4,5},{7,6},{8,9},{11,10},{12,13},{15,14},{16,17},{19,... | collective-permute-start | bytes 1966088 | tf_op jit(solution)/shard_map/ppermute | solution.py:260
  32.4 24.9 %collective-permute-start.11 = (bf16[32,5120]{1,0:T(8,128)(2,1)S(1)}, bf16[32,5120]{1,0:T(8,128)(2,1)S(1)}, u32[]{:S(2)}, u32[]{:S(2)}) collective-permute-start(bf16[32,5120]{1,0:T(8,128)(2,1)S(1)} %get-tuple-element.29), channel_id=1, source_target_pairs={{1,2},{2,1},{5,6},{6,5},{9,10},{10,9},{13,14},{14,13},{17,18},{18,... | collective-permute-start | bytes 983048 | tf_op jit(solution)/shard_map/ppermute | solution.py:270
  34.8 22.6 %collective-permute-start.10 = (bf16[32,5120]{1,0:T(8,128)(2,1)S(1)}, bf16[32,5120]{1,0:T(8,128)(2,1)S(1)}, u32[]{:S(2)}, u32[]{:S(2)}) collective-permute-start(bf16[32,5120]{1,0:T(8,128)(2,1)S(1)} %get-tuple-element.29), channel_id=1, source_target_pairs={{0,2},{3,1},{4,6},{7,5},{8,10},{11,9},{12,14},{15,13},{16,18},{19,... | collective-permute-start | bytes 983048 | tf_op jit(solution)/shard_map/ppermute | solution.py:267
  36.1 21.3 %collective-permute-start.12 = (bf16[32,5120]{1,0:T(8,128)(2,1)S(1)}, bf16[32,5120]{1,0:T(8,128)(2,1)S(1)}, u32[]{:S(2)}, u32[]{:S(2)}) collective-permute-start(bf16[32,5120]{1,0:T(8,128)(2,1)S(1)} %get-tuple-element.30), channel_id=1, source_target_pairs={{0,1},{3,2},{4,5},{7,6},{8,9},{11,10},{12,13},{15,14},{16,17},{19,... | collective-permute-start | bytes 983048 | tf_op jit(solution)/shard_map/ppermute | solution.py:268
  37.4 33.6 %collective-permute-start.7 = (bf16[64,5120]{1,0:T(8,128)(2,1)S(1)}, bf16[64,5120]{1,0:T(8,128)(2,1)S(1)}, u32[]{:S(2)}, u32[]{:S(2)}) collective-permute-start(bf16[64,5120]{1,0:T(8,128)(2,1)S(1)} %get-tuple-element.22), channel_id=1, source_target_pairs={{0,1},{1,0},{2,3},{3,2},{4,5},{5,4},{6,7},{7,6},{8,9},{9,8},{10,11... | collective-permute-start | bytes 1966088 | tf_op jit(solution)/shard_map/ppermute | solution.py:269
  43.4 29.2 %collective-permute-start.9 = (bf16[64,5120]{1,0:T(8,128)(2,1)S(1)}, bf16[64,5120]{1,0:T(8,128)(2,1)S(1)}, u32[]{:S(2)}, u32[]{:S(2)}) collective-permute-start(bf16[64,5120]{1,0:T(8,128)(2,1)S(1)} %add_convert_fusion), channel_id=1, source_target_pairs={{1,3},{2,0},{5,7},{6,4},{9,11},{10,8},{13,15},{14,12},{17,19},{18,... | collective-permute-start | bytes 1966088 | tf_op jit(solution)/shard_map/ppermute | solution.py:272
  57.5 15.1 %collective-permute-start.13 = (bf16[32,5120]{1,0:T(8,128)(2,1)S(1)}, bf16[32,5120]{1,0:T(8,128)(2,1)S(1)}, u32[]{:S(2)}, u32[]{:S(2)}) collective-permute-start(bf16[32,5120]{1,0:T(8,128)(2,1)S(1)} %add_convert_fusion.2), channel_id=1, source_target_pairs={{1,2},{2,1},{5,6},{6,5},{9,10},{10,9},{13,14},{14,13},{17,18},{18,... | collective-permute-start | bytes 983048 | tf_op jit(solution)/shard_map/ppermute | solution.py:274

commit v4 on v3

--- a/solution.py
+++ b/solution.py
@@ -76,7 +76,7 @@
         copy.wait()
 
 
-def layer_kernel(q_ref, *refs, heads, per_kv, chips, order, hops, first, last):
+def layer_kernel(q_ref, *refs, heads, per_kv, chips, order, outer, hops, first, last):
     chunks = len(order)
     count = 2 * first + len(hops)
     kv_ref, refs = refs[:count], refs[count:]
@@ -96,8 +96,13 @@
     there = [pl.ds(start, rows) for start in starts]
     here = [slice(i * rows, (i + 1) * rows) for i in range(chunks)]
 
-    def every(step):
-        for i in range(chunks):
+    def run(begin):
+        attend(range(begin, chunks))
+        if last:
+            project(range(begin, chunks))
+
+    def every(step, todo):
+        for i in todo:
             for g in range(kv_here):
                 mine = range(g * per_kv, (g + 1) * per_kv)
                 step(i, g, jnp.concatenate([q_ref[there[i], head(h)] for h in mine], axis=0))
@@ -117,42 +122,69 @@
             query, keys_of(seen, g), values_of(seen, g, kv_here), acc_ref[i, g], top_ref[i, g]
         )
 
-    if first:
-        every(own)
-    else:
-        acc_ref[...] = acc_in[...]
-        top_ref[...] = top_in[...]
     blocks = kv_ref[2 * first :]
     bits = sorted({d.bit_length() - 1 for d in hops})
     some = {bit: [x for d, x in zip(hops, blocks) if d.bit_length() - 1 == bit] for bit in bits}
     seen = {bit: (chip >> bit) & 1 == 1 for bit in bits}
 
-    def add(case, group):
-        pl.when(case)(functools.partial(every, functools.partial(others, seen=group)))
-
-    if len(hops) <= GROUP and len(bits) == 2:
-        low, high = bits
-        add(seen[low] & seen[high], some[high] + some[low])
-        add(seen[low] & ~seen[high], some[low])
-        add(~seen[low] & seen[high], some[high])
-    else:
-        for bit in bits:
-            for at in range(0, len(some[bit]), GROUP):
-                add(seen[bit], some[bit][at : at + GROUP])
-    if not last:
+    def attend(todo):
+        if first:
+            every(own, todo)
+        else:
+            acc_ref[...] = acc_in[...]
+            top_ref[...] = top_in[...]
+
+        def add(case, group):
+            step = functools.partial(others, seen=group)
+            pl.when(case)(functools.partial(every, step, todo))
+
+        if len(hops) <= GROUP and len(bits) == 2:
+            low, high = bits
+            add(seen[low] & seen[high], some[high] + some[low])
+            add(seen[low] & ~seen[high], some[low])
+            add(~seen[low] & seen[high], some[high])
+        else:
+            for bit in bits:
+                for at in range(0, len(some[bit]), GROUP):
+                    add(seen[bit], some[bit][at : at + GROUP])
+
+    def project(todo):
+        for i in todo:
+            for h in range(heads):
+                g, j = h // per_kv, h % per_kv
+                state = acc_ref[i, g, j * rows : (j + 1) * rows, :]
+                att_ref[here[i], head(h)] = (
+                    state[:, :HEAD_DIMENSION] / state[:, HEAD_DIMENSION:]
+                ).astype(jnp.bfloat16)
+        attended = att_ref[todo[0] * rows :, :]
+        for at in range(0, w_ref.shape[1], TILE):
+            part = dot(attended, w_ref[:, at : at + TILE]).astype(jnp.bfloat16)
+            for j, i in enumerate(todo):
+                outs[i][:, at : at + TILE] = part[here[j]]
+
+    if len(set(outer)) == 1:
+        run(outer[0])
         return
-    for i in range(chunks):
-        for h in range(heads):
-            g, j = h // per_kv, h % per_kv
-            state = acc_ref[i, g, j * rows : (j + 1) * rows, :]
-            att_ref[here[i], head(h)] = (
-                state[:, :HEAD_DIMENSION] / state[:, HEAD_DIMENSION:]
-            ).astype(jnp.bfloat16)
-    attended = att_ref[...]
-    for at in range(0, w_ref.shape[1], TILE):
-        part = dot(attended, w_ref[:, at : at + TILE]).astype(jnp.bfloat16)
-        for i in range(chunks):
-            outs[i][:, at : at + TILE] = part[here[i]]
+    is_outer = (tp_at == 0) | (tp_at == 3)
+    for case, begin in ((is_outer, outer[0]), (~is_outer, outer[1])):
+        if begin < chunks:
+            pl.when(case)(functools.partial(run, begin))
+        for out in outs[:begin] if last else []:
+
+            @pl.when(case)
+            def _(out=out):
+                out[...] = jnp.zeros_like(out)
+
+
+def add_kernel(*refs, half):
+    *terms, out = refs
+    mine, side, far, direct, early, late = terms
+    for rows, more in ((slice(0, half), [direct, early]), (slice(half, 2 * half), [late])):
+        total = mine[rows].astype(jnp.float32) + side[rows].astype(jnp.float32)
+        total = total + far[rows].astype(jnp.float32)
+        for term in more:
+            total = total + term[...].astype(jnp.float32)
+        out[rows] = total.astype(out.dtype)
 
 
 def call(kernel, out_shape, *args, scratch, limit, place=pltpu.VMEM):
@@ -218,7 +250,7 @@
     swapped = [lax.ppermute(block, "seq", swap) for block in blocks]
     hops = list(range(1, chips))
 
-    def layer(order, rows, seen, state=None, first=True, last=True):
+    def layer(order, rows, seen, state=None, first=True, last=True, outer=(0, 0)):
         chunks = len(order)
         running = [(chunks, kv_here, per_kv * rows, 2 * hd), (chunks, kv_here, per_kv * rows, hd)]
         own_blocks = [own, swapped[0]] if first else []
@@ -230,6 +262,7 @@
                 per_kv=per_kv,
                 chips=chips,
                 order=order,
+                outer=outer,
                 hops=[d for d, _ in seen],
                 first=first,
                 last=last,
@@ -254,12 +287,15 @@
 
     rows = tok // 4
     far_rows = [lambda at: jnp.where(at < 2, 3, 0)]
-    state = layer(far_rows, rows, got, last=False)
-    (far,) = layer(far_rows, rows, theirs, state, first=False)
+    state = layer(far_rows, rows, got, last=False, outer=(0, 1))
+    (far,) = layer(far_rows, rows, theirs, state, first=False, outer=(0, 1))
     inward, sides = [(0, 1), (3, 2)], [(0, 1), (1, 0), (2, 3), (3, 2)]
     got_far = lax.ppermute(far, "tp", inward)
-    near, side, mine = layer(
-        [lambda at: jnp.where(at < 2, 2, 1), lambda at: at ^ 1, lambda at: at], rows, got + theirs
+    far_here, near, side, mine = layer(
+        far_rows + [lambda at: jnp.where(at < 2, 2, 1), lambda at: at ^ 1, lambda at: at],
+        rows,
+        got + theirs,
+        outer=(1, 0),
     )
     half = rows // 2
     early, late = near[:half], near[half:]
@@ -268,17 +304,23 @@
     got_late = lax.ppermute(late, "tp", inward)
     got_side = lax.ppermute(side, "tp", sides)
     got_early = lax.ppermute(early, "tp", outward)
-    total_far = added(got_far, far)
+    total_far = added(got_far, far_here)
     across_far = lax.ppermute(total_far, "tp", [(1, 3), (2, 0)])
     got_late = after(got_late, got_direct, got_early, total_far)
     across_late = lax.ppermute(added(got_late, late), "tp", outward)
-    return jnp.concatenate(
-        [
-            added(mine[:half], got_side[:half], across_far[:half], got_direct, got_early),
-            added(mine[half:], got_side[half:], across_far[half:], across_late),
-        ],
-        axis=0,
-    )
+    (out,) = call(
+        functools.partial(add_kernel, half=half),
+        [jax.ShapeDtypeStruct(mine.shape, mine.dtype)],
+        mine,
+        got_side,
+        across_far,
+        got_direct,
+        got_early,
+        across_late,
+        scratch=[],
+        limit=24,
+    )
+    return out
 
 
 def solution(mesh):

time: 74.1 us -> 73 us (0.985)
  waiting for transfers between devices: 35.4 us -> 37.2 us
  Pallas kernels: 14.6 us -> 12.9 us
  other arithmetic: 1.48 us -> 0.23 us
    ppermute x4, waiting for transfers between devices: 0.01 us -> 1.74 us  [body(): swapped = [lax.ppermute(block, 'seq', swap) for block in blocks]]
    pallas_call x5 -> x6, Pallas kernels: 14.6 us -> 12.9 us  [call(): pl.pallas_call(kernel, out_shape=out_shape, in_specs=[pl.BlockSpec(memory...]
    concatenate x1 -> x0, other arithmetic: 0.88 us -> none  [body(): jnp.concatenate([added(mine[:half], got_side[:half], across_far[:half], g...]
  transfers between devices with their start and end apart: 14 -> 14, of which waited for: 6 -> 9; matrix products, arithmetic and copies ran while one was open for 0% -> 0% of each run, Pallas kernels for 13% -> 14%
where the time goes in v4:
time: 73 us; the launch traced here: 72.3 us
  waiting for transfers between devices  37.2 us (51%)
  starting transfers between devices  17.7 us (24%)
  Pallas kernels  12.9 us (18%)
  local copies, waits for them, and re-layouts  4.03 us (6%)
    pallas_call x6, Pallas kernels, call(): pl.pallas_call(kernel, out_shape=out_shape, in_specs=[pl.BlockSpec(memory...  12.9 us
    ppermute x1, waiting for transfers between devices, body(): got_late = lax.ppermute(late, 'tp', inward)  12.6 us
    ppermute x1, waiting for transfers between devices, body(): got_side = lax.ppermute(side, 'tp', sides)  11.8 us
    ppermute x3, waiting for transfers between devices, body(): blocks.append(lax.ppermute(own, 'seq', pairs))  7.94 us
    unnamed x6, local copies, waits for them, and re-layouts  3.98 us
    ppermute x3, starting transfers between devices, body(): blocks.append(lax.ppermute(own, 'seq', pairs))  3.88 us
    ppermute x1, starting transfers between devices, body(): got_side = lax.ppermute(side, 'tp', sides)  3.76 us
    ppermute x1, starting transfers between devices, body(): got_early = lax.ppermute(early, 'tp', outward)  2.36 us
  transfers between devices with their start and end apart: 14, of which 9 were waited for; matrix products, arithmetic and copies ran while one was open for 0% of the time, Pallas kernels for 14%

profile of v4, /device:TPU:22, one launch (start us, length us, event | category | flops | bytes accessed | tf_op | source)
XLA Modules:
  0.0 72.3 jit_solution(3114468591097966220)
XLA Ops:
  0.0 1.7 %shard_map.47.refs_0_ = bf16[256,512]{1,0:T(8,128)(2,1)} custom-call(bf16[256,1024]{1,0:T(8,128)(2,1)} %keys.1, bf16[256,1024]{1,0:T(8,128)(2,1)} %values.1), custom_call_target="tpu_custom_call" | custom-call | tf_op jit(solution)/shard_map/pallas_call | solution.py:191
  1.8 1.3 %collective-permute-start.3 = (bf16[256,512]{1,0:T(8,128)(2,1)}, bf16[256,512]{1,0:T(8,128)(2,1)S(1)}, u32[]{:S(2)}, u32[]{:S(2)}) collective-permute-start(bf16[256,512]{1,0:T(8,128)(2,1)} %shard_map.47.refs_0_), channel_id=1, source_target_pairs={{0,24},{4,28},{8,16},{12,20},{1,25},{5,29},{9,17},{13,21},{2,26},{... | collective-permute-start | bytes 786440 | tf_op jit(solution)/shard_map/ppermute | solution.py:239
  3.1 1.3 %collective-permute-start.2 = (bf16[256,512]{1,0:T(8,128)(2,1)}, bf16[256,512]{1,0:T(8,128)(2,1)S(1)}, u32[]{:S(2)}, u32[]{:S(2)}) collective-permute-start(bf16[256,512]{1,0:T(8,128)(2,1)} %shard_map.47.refs_0_), channel_id=1, source_target_pairs={{0,16},{4,20},{8,24},{12,28},{1,17},{5,21},{9,25},{13,29},{2,18},{... | collective-permute-start | bytes 786440 | tf_op jit(solution)/shard_map/ppermute | solution.py:239
  4.4 1.3 %collective-permute-start.1 = (bf16[256,512]{1,0:T(8,128)(2,1)}, bf16[256,512]{1,0:T(8,128)(2,1)S(1)}, u32[]{:S(2)}, u32[]{:S(2)}) collective-permute-start(bf16[256,512]{1,0:T(8,128)(2,1)} %shard_map.47.refs_0_), channel_id=1, source_target_pairs={{0,8},{4,12},{16,24},{20,28},{1,9},{5,13},{17,25},{21,29},{2,10},{... | collective-permute-start | bytes 786440 | tf_op jit(solution)/shard_map/ppermute | solution.py:239
  5.7 0.1 collective-permute-start
  5.7 0.0 copy-start
  5.8 4.0 %copy-done = bf16[1024,5120]{1,0:T(8,128)(2,1)S(1)} copy-done((bf16[1024,5120]{1,0:T(8,128)(2,1)S(1)}, bf16[1024,5120]{1,0:T(8,128)(2,1)}, u32[]{:S(2)}) %copy-start) | copy-done | bytes 10485784
  9.7 0.8 %shard_map.46 = (bf16[256,1024]{1,0:T(8,128)(2,1)S(1)}, bf16[1024,5120]{1,0:T(8,128)(2,1)S(1)}) custom-call(bf16[256,1024]{1,0:T(8,128)(2,1)S(1)} %copy-done.2, bf16[1024,5120]{1,0:T(8,128)(2,1)S(1)} %copy-done), custom_call_target="tpu_custom_call" | custom-call | tf_op jit(solution)/shard_map/pallas_call | solution.py:191
  10.5 3.5 %collective-permute-done.3.refs_4_ = bf16[256,512]{1,0:T(8,128)(2,1)S(1)} collective-permute-done((bf16[256,512]{1,0:T(8,128)(2,1)}, bf16[256,512]{1,0:T(8,128)(2,1)S(1)}, u32[]{:S(2)}, u32[]{:S(2)}) %collective-permute-start.3) | collective-permute-done | bytes 262176 | tf_op jit(solution)/shard_map/ppermute | solution.py:239
  14.0 4.4 %collective-permute-done.2.refs_3_ = bf16[256,512]{1,0:T(8,128)(2,1)S(1)} collective-permute-done((bf16[256,512]{1,0:T(8,128)(2,1)}, bf16[256,512]{1,0:T(8,128)(2,1)S(1)}, u32[]{:S(2)}, u32[]{:S(2)}) %collective-permute-start.2) | collective-permute-done | bytes 262176 | tf_op jit(solution)/shard_map/ppermute | solution.py:239
  18.4 0.0 collective-permute-done.1.refs_2_
  18.4 0.0 collective-permute-start.4
  18.4 0.5 collective-permute-start.5
  18.9 0.0 collective-permute-start.6
  19.0 1.0 %collective-permute-done.4.refs_5_.refs_0_ = bf16[256,512]{1,0:T(8,128)(2,1)S(1)} collective-permute-done((bf16[256,512]{1,0:T(8,128)(2,1)S(1)}, bf16[256,512]{1,0:T(8,128)(2,1)S(1)}, u32[]{:S(2)}, u32[]{:S(2)}) %collective-permute-start.4) | collective-permute-done | bytes 262176 | tf_op jit(solution)/shard_map/ppermute | solution.py:250
  20.0 0.4 collective-permute-done.5.refs_6_.refs_1_
  20.3 0.4 collective-permute-done.6.refs_7_.refs_2_
  20.8 1.3 %collective-permute-start.8 = (bf16[64,5120]{1,0:T(8,128)(2,1)S(1)}, bf16[64,5120]{1,0:T(8,128)(2,1)S(1)}, u32[]{:S(2)}, u32[]{:S(2)}) collective-permute-start(bf16[64,5120]{1,0:T(8,128)(2,1)S(1)} %shard_map.50), channel_id=1, source_target_pairs={{0,1},{3,2},{4,5},{7,6},{8,9},{11,10},{12,13},{15,14},{16,17},{19,... | collective-permute-start | bytes 1966088 | tf_op jit(solution)/shard_map/ppermute | solution.py:293
  22.1 9.2 %shard_map.48 = (bf16[64,5120]{1,0:T(8,128)(2,1)S(1)}, bf16[64,5120]{1,0:T(8,128)(2,1)S(1)}, bf16[64,5120]{1,0:T(8,128)(2,1)S(1)}, bf16[64,5120]{1,0:T(8,128)(2,1)S(1)}) custom-call(bf16[256,1024]{1,0:T(8,128)(2,1)S(1)} %get-tuple-element.17.q_ref, bf16[256,512]{1,0:T(8,128)(2,1)S(1)} %copy-done.1, bf16[256,512]{1,0:T(8,128)(2,1)S(1)} %collective-permute-done.refs_1_, ...), custom_call_target="tpu_custom_call" | custom-call | tf_op jit(solution)/shard_map/pallas_call | solution.py:191
  31.3 2.4 %collective-permute-start.11 = (bf16[32,5120]{1,0:T(8,128)(2,1)S(1)}, bf16[32,5120]{1,0:T(8,128)(2,1)S(1)}, u32[]{:S(2)}, u32[]{:S(2)}) collective-permute-start(bf16[32,5120]{1,0:T(8,128)(2,1)S(1)} %get-tuple-element.30), channel_id=1, source_target_pairs={{1,2},{2,1},{5,6},{6,5},{9,10},{10,9},{13,14},{14,13},{17,18},{18,... | collective-permute-start | bytes 983048 | tf_op jit(solution)/shard_map/ppermute | solution.py:306
  33.7 1.3 %collective-permute-start.10 = (bf16[32,5120]{1,0:T(8,128)(2,1)S(1)}, bf16[32,5120]{1,0:T(8,128)(2,1)S(1)}, u32[]{:S(2)}, u32[]{:S(2)}) collective-permute-start(bf16[32,5120]{1,0:T(8,128)(2,1)S(1)} %get-tuple-element.30), channel_id=1, source_target_pairs={{0,2},{3,1},{4,6},{7,5},{8,10},{11,9},{12,14},{15,13},{16,18},{19,... | collective-permute-start | bytes 983048 | tf_op jit(solution)/shard_map/ppermute | solution.py:303
  35.0 1.3 %collective-permute-start.12 = (bf16[32,5120]{1,0:T(8,128)(2,1)S(1)}, bf16[32,5120]{1,0:T(8,128)(2,1)S(1)}, u32[]{:S(2)}, u32[]{:S(2)}) collective-permute-start(bf16[32,5120]{1,0:T(8,128)(2,1)S(1)} %get-tuple-element.29), channel_id=1, source_target_pairs={{0,1},{3,2},{4,5},{7,6},{8,9},{11,10},{12,13},{15,14},{16,17},{19,... | collective-permute-start | bytes 983048 | tf_op jit(solution)/shard_map/ppermute | solution.py:304
  36.3 3.8 %collective-permute-start.7 = (bf16[64,5120]{1,0:T(8,128)(2,1)S(1)}, bf16[64,5120]{1,0:T(8,128)(2,1)S(1)}, u32[]{:S(2)}, u32[]{:S(2)}) collective-permute-start(bf16[64,5120]{1,0:T(8,128)(2,1)S(1)} %get-tuple-element.23), channel_id=1, source_target_pairs={{0,1},{1,0},{2,3},{3,2},{4,5},{5,4},{6,7},{7,6},{8,9},{9,8},{10,11... | collective-permute-start | bytes 1966088 | tf_op jit(solution)/shard_map/ppermute | solution.py:305
  40.0 2.3 %collective-permute-done.8 = bf16[64,5120]{1,0:T(8,128)(2,1)S(1)} collective-permute-done((bf16[64,5120]{1,0:T(8,128)(2,1)S(1)}, bf16[64,5120]{1,0:T(8,128)(2,1)S(1)}, u32[]{:S(2)}, u32[]{:S(2)}) %collective-permute-start.8) | collective-permute-done | bytes 655392 | tf_op jit(solution)/shard_map/ppermute | solution.py:293
  42.3 0.2 add_convert_fusion
  42.5 1.3 %collective-permute-start.9 = (bf16[64,5120]{1,0:T(8,128)(2,1)S(1)}, bf16[64,5120]{1,0:T(8,128)(2,1)S(1)}, u32[]{:S(2)}, u32[]{:S(2)}) collective-permute-start(bf16[64,5120]{1,0:T(8,128)(2,1)S(1)} %add_convert_fusion), channel_id=1, source_target_pairs={{1,3},{2,0},{5,7},{6,4},{9,11},{10,8},{13,15},{14,12},{17,19},{18,... | collective-permute-start | bytes 1966088 | tf_op jit(solution)/shard_map/ppermute | solution.py:308
  43.8 12.6 %collective-permute-done.12 = bf16[32,5120]{1,0:T(8,128)(2,1)S(1)} collective-permute-done((bf16[32,5120]{1,0:T(8,128)(2,1)S(1)}, bf16[32,5120]{1,0:T(8,128)(2,1)S(1)}, u32[]{:S(2)}, u32[]{:S(2)}) %collective-permute-start.12) | collective-permute-done | bytes 327712 | tf_op jit(solution)/shard_map/ppermute | solution.py:304
  56.4 0.1 add_convert_fusion.1
  56.5 1.9 %collective-permute-start.13 = (bf16[32,5120]{1,0:T(8,128)(2,1)S(1)}, bf16[32,5120]{1,0:T(8,128)(2,1)S(1)}, u32[]{:S(2)}, u32[]{:S(2)}) collective-permute-start(bf16[32,5120]{1,0:T(8,128)(2,1)S(1)} %add_convert_fusion.1), channel_id=1, source_target_pairs={{1,2},{2,1},{5,6},{6,5},{9,10},{10,9},{13,14},{14,13},{17,18},{18,... | collective-permute-start | bytes 983048 | tf_op jit(solution)/shard_map/ppermute | solution.py:310
  58.4 11.8 %collective-permute-done.7.refs_1_ = bf16[64,5120]{1,0:T(8,128)(2,1)S(1)} collective-permute-done((bf16[64,5120]{1,0:T(8,128)(2,1)S(1)}, bf16[64,5120]{1,0:T(8,128)(2,1)S(1)}, u32[]{:S(2)}, u32[]{:S(2)}) %collective-permute-start.7) | collective-permute-done | bytes 655392 | tf_op jit(solution)/shard_map/ppermute | solution.py:305
  70.2 0.8 %collective-permute-done.13.refs_5_ = bf16[32,5120]{1,0:T(8,128)(2,1)S(1)} collective-permute-done((bf16[32,5120]{1,0:T(8,128)(2,1)S(1)}, bf16[32,5120]{1,0:T(8,128)(2,1)S(1)}, u32[]{:S(2)}, u32[]{:S(2)}) %collective-permute-start.13) | collective-permute-done | bytes 327712 | tf_op jit(solution)/shard_map/ppermute | solution.py:310
  71.1 1.2 %shard_map.51 = bf16[64,5120]{1,0:T(8,128)(2,1)} custom-call(bf16[64,5120]{1,0:T(8,128)(2,1)S(1)} %get-tuple-element.22.refs_0_, bf16[64,5120]{1,0:T(8,128)(2,1)S(1)} %collective-permute-done.7.refs_1_, bf16[64,5120]{1,0:T(8,128)(2,1)S(1)} %collective-permute-done.9.refs_2_, bf16[32,5120]{1,0:T(8,128)(2,1)S(1)} %collective-permute-done.10.refs_3_, ...), custom_call_target="tpu_custom_call" | custom-call | tf_op jit(solution)/shard_map/pallas_call | solution.py:191
  (11 shorter events, 0.1 us)
Async XLA Ops:
  0.0 5.7 %copy-start.2 = (bf16[256,1024]{1,0:T(8,128)(2,1)S(1)}, bf16[256,1024]{1,0:T(8,128)(2,1)}, u32[]{:S(2)}) copy-start(bf16[256,1024]{1,0:T(8,128)(2,1)} %refs_0_.1) | copy-start | bytes 1572868
  1.8 12.2 %collective-permute-start.3 = (bf16[256,512]{1,0:T(8,128)(2,1)}, bf16[256,512]{1,0:T(8,128)(2,1)S(1)}, u32[]{:S(2)}, u32[]{:S(2)}) collective-permute-start(bf16[256,512]{1,0:T(8,128)(2,1)} %shard_map.47.refs_0_), channel_id=1, source_target_pairs={{0,24},{4,28},{8,16},{12,20},{1,25},{5,29},{9,17},{13,21},{2,26},{... | collective-permute-start | bytes 786440 | tf_op jit(solution)/shard_map/ppermute | solution.py:239
  3.1 15.4 %collective-permute-start.2 = (bf16[256,512]{1,0:T(8,128)(2,1)}, bf16[256,512]{1,0:T(8,128)(2,1)S(1)}, u32[]{:S(2)}, u32[]{:S(2)}) collective-permute-start(bf16[256,512]{1,0:T(8,128)(2,1)} %shard_map.47.refs_0_), channel_id=1, source_target_pairs={{0,16},{4,20},{8,24},{12,28},{1,17},{5,21},{9,25},{13,29},{2,18},{... | collective-permute-start | bytes 786440 | tf_op jit(solution)/shard_map/ppermute | solution.py:239
  4.4 14.1 %collective-permute-start.1 = (bf16[256,512]{1,0:T(8,128)(2,1)}, bf16[256,512]{1,0:T(8,128)(2,1)S(1)}, u32[]{:S(2)}, u32[]{:S(2)}) collective-permute-start(bf16[256,512]{1,0:T(8,128)(2,1)} %shard_map.47.refs_0_), channel_id=1, source_target_pairs={{0,8},{4,12},{16,24},{20,28},{1,9},{5,13},{17,25},{21,29},{2,10},{... | collective-permute-start | bytes 786440 | tf_op jit(solution)/shard_map/ppermute | solution.py:239
  5.7 13.3 %collective-permute-start = (bf16[256,512]{1,0:T(8,128)(2,1)}, bf16[256,512]{1,0:T(8,128)(2,1)S(1)}, u32[]{:S(2)}, u32[]{:S(2)}) collective-permute-start(bf16[256,512]{1,0:T(8,128)(2,1)} %shard_map.47.refs_0_), channel_id=1, source_target_pairs={{0,4},{4,0},{8,12},{12,8},{16,20},{20,16},{24,28},{28,24},{1,5},{5... | collective-permute-start | bytes 786440 | tf_op jit(solution)/shard_map/ppermute | solution.py:250
  5.7 4.0 %copy-start = (bf16[1024,5120]{1,0:T(8,128)(2,1)S(1)}, bf16[1024,5120]{1,0:T(8,128)(2,1)}, u32[]{:S(2)}) copy-start(bf16[1024,5120]{1,0:T(8,128)(2,1)} %refs_1_.1) | copy-start | bytes 31457284
  9.7 9.2 %copy-start.1 = (bf16[256,512]{1,0:T(8,128)(2,1)S(1)}, bf16[256,512]{1,0:T(8,128)(2,1)}, u32[]{:S(2)}) copy-start(bf16[256,512]{1,0:T(8,128)(2,1)} %shard_map.47.refs_0_) | copy-start | bytes 786436
  18.4 1.5 %collective-permute-start.4 = (bf16[256,512]{1,0:T(8,128)(2,1)S(1)}, bf16[256,512]{1,0:T(8,128)(2,1)S(1)}, u32[]{:S(2)}, u32[]{:S(2)}) collective-permute-start(bf16[256,512]{1,0:T(8,128)(2,1)S(1)} %collective-permute-done.1.refs_2_), channel_id=1, source_target_pairs={{0,4},{4,0},{8,12},{12,8},{16,20},{20,16},{24,28},{28,24},{1,5},{5... | collective-permute-start | bytes 786440 | tf_op jit(solution)/shard_map/ppermute | solution.py:250
  18.4 1.9 %collective-permute-start.5 = (bf16[256,512]{1,0:T(8,128)(2,1)S(1)}, bf16[256,512]{1,0:T(8,128)(2,1)S(1)}, u32[]{:S(2)}, u32[]{:S(2)}) collective-permute-start(bf16[256,512]{1,0:T(8,128)(2,1)S(1)} %collective-permute-done.2.refs_3_), channel_id=1, source_target_pairs={{0,4},{4,0},{8,12},{12,8},{16,20},{20,16},{24,28},{28,24},{1,5},{5... | collective-permute-start | bytes 786440 | tf_op jit(solution)/shard_map/ppermute | solution.py:250
  18.9 1.8 %collective-permute-start.6 = (bf16[256,512]{1,0:T(8,128)(2,1)S(1)}, bf16[256,512]{1,0:T(8,128)(2,1)S(1)}, u32[]{:S(2)}, u32[]{:S(2)}) collective-permute-start(bf16[256,512]{1,0:T(8,128)(2,1)S(1)} %collective-permute-done.3.refs_4_), channel_id=1, source_target_pairs={{0,4},{4,0},{8,12},{12,8},{16,20},{20,16},{24,28},{28,24},{1,5},{5... | collective-permute-start | bytes 786440 | tf_op jit(solution)/shard_map/ppermute | solution.py:250
  20.8 21.5 %collective-permute-start.8 = (bf16[64,5120]{1,0:T(8,128)(2,1)S(1)}, bf16[64,5120]{1,0:T(8,128)(2,1)S(1)}, u32[]{:S(2)}, u32[]{:S(2)}) collective-permute-start(bf16[64,5120]{1,0:T(8,128)(2,1)S(1)} %shard_map.50), channel_id=1, source_target_pairs={{0,1},{3,2},{4,5},{7,6},{8,9},{11,10},{12,13},{15,14},{16,17},{19,... | collective-permute-start | bytes 1966088 | tf_op jit(solution)/shard_map/ppermute | solution.py:293
  31.3 25.1 %collective-permute-start.11 = (bf16[32,5120]{1,0:T(8,128)(2,1)S(1)}, bf16[32,5120]{1,0:T(8,128)(2,1)S(1)}, u32[]{:S(2)}, u32[]{:S(2)}) collective-permute-start(bf16[32,5120]{1,0:T(8,128)(2,1)S(1)} %get-tuple-element.30), channel_id=1, source_target_pairs={{1,2},{2,1},{5,6},{6,5},{9,10},{10,9},{13,14},{14,13},{17,18},{18,... | collective-permute-start | bytes 983048 | tf_op jit(solution)/shard_map/ppermute | solution.py:306
  33.7 22.7 %collective-permute-start.10 = (bf16[32,5120]{1,0:T(8,128)(2,1)S(1)}, bf16[32,5120]{1,0:T(8,128)(2,1)S(1)}, u32[]{:S(2)}, u32[]{:S(2)}) collective-permute-start(bf16[32,5120]{1,0:T(8,128)(2,1)S(1)} %get-tuple-element.30), channel_id=1, source_target_pairs={{0,2},{3,1},{4,6},{7,5},{8,10},{11,9},{12,14},{15,13},{16,18},{19,... | collective-permute-start | bytes 983048 | tf_op jit(solution)/shard_map/ppermute | solution.py:303
  35.0 21.4 %collective-permute-start.12 = (bf16[32,5120]{1,0:T(8,128)(2,1)S(1)}, bf16[32,5120]{1,0:T(8,128)(2,1)S(1)}, u32[]{:S(2)}, u32[]{:S(2)}) collective-permute-start(bf16[32,5120]{1,0:T(8,128)(2,1)S(1)} %get-tuple-element.29), channel_id=1, source_target_pairs={{0,1},{3,2},{4,5},{7,6},{8,9},{11,10},{12,13},{15,14},{16,17},{19,... | collective-permute-start | bytes 983048 | tf_op jit(solution)/shard_map/ppermute | solution.py:304
  36.3 34.0 %collective-permute-start.7 = (bf16[64,5120]{1,0:T(8,128)(2,1)S(1)}, bf16[64,5120]{1,0:T(8,128)(2,1)S(1)}, u32[]{:S(2)}, u32[]{:S(2)}) collective-permute-start(bf16[64,5120]{1,0:T(8,128)(2,1)S(1)} %get-tuple-element.23), channel_id=1, source_target_pairs={{0,1},{1,0},{2,3},{3,2},{4,5},{5,4},{6,7},{7,6},{8,9},{9,8},{10,11... | collective-permute-start | bytes 1966088 | tf_op jit(solution)/shard_map/ppermute | solution.py:305
  42.5 28.6 %collective-permute-start.9 = (bf16[64,5120]{1,0:T(8,128)(2,1)S(1)}, bf16[64,5120]{1,0:T(8,128)(2,1)S(1)}, u32[]{:S(2)}, u32[]{:S(2)}) collective-permute-start(bf16[64,5120]{1,0:T(8,128)(2,1)S(1)} %add_convert_fusion), channel_id=1, source_target_pairs={{1,3},{2,0},{5,7},{6,4},{9,11},{10,8},{13,15},{14,12},{17,19},{18,... | collective-permute-start | bytes 1966088 | tf_op jit(solution)/shard_map/ppermute | solution.py:308
  56.5 14.6 %collective-permute-start.13 = (bf16[32,5120]{1,0:T(8,128)(2,1)S(1)}, bf16[32,5120]{1,0:T(8,128)(2,1)S(1)}, u32[]{:S(2)}, u32[]{:S(2)}) collective-permute-start(bf16[32,5120]{1,0:T(8,128)(2,1)S(1)} %add_convert_fusion.1), channel_id=1, source_target_pairs={{1,2},{2,1},{5,6},{6,5},{9,10},{10,9},{13,14},{14,13},{17,18},{18,... | collective-permute-start | bytes 983048 | tf_op jit(solution)/shard_map/ppermute | solution.py:310

commit v5 on v4

--- a/solution.py
+++ b/solution.py
@@ -16,6 +16,7 @@
 NEGATIVE = -1e30
 TILE = 512
 GROUP = 6
+ROWS = 16
 
 
 def dot(a, b):
@@ -76,14 +77,19 @@
         copy.wait()
 
 
-def layer_kernel(q_ref, *refs, heads, per_kv, chips, order, outer, hops, first, last):
+def layer_kernel(q_ref, *refs, heads, per_kv, chips, order, outer, hops, first, last, split=None, upto=None):
     chunks = len(order)
     count = 2 * first + len(hops)
     kv_ref, refs = refs[:count], refs[count:]
     if not first:
         acc_in, top_in, refs = refs[0], refs[1], refs[2:]
     if last:
-        w_ref, outs, (acc_ref, top_ref, att_ref) = refs[0], refs[1 : 1 + chunks], refs[1 + chunks :]
+        w_ref, outs, (acc_ref, top_ref, att_ref) = refs[0], list(refs[1:-3]), refs[-3:]
+        if upto:
+            outs, att_ref, acc_ref, top_ref = outs[:-1], outs[-1], *refs[-3:-1]
+        if split:
+            chunk, column = split
+            outs[chunk : chunk + 2] = [(outs[chunk], outs[chunk + 1])]
     else:
         acc_ref, top_ref = refs
     rows = acc_ref.shape[2] // per_kv
@@ -157,10 +163,13 @@
                     state[:, :HEAD_DIMENSION] / state[:, HEAD_DIMENSION:]
                 ).astype(jnp.bfloat16)
         attended = att_ref[todo[0] * rows :, :]
-        for at in range(0, w_ref.shape[1], TILE):
+        for at in range(0, upto or w_ref.shape[1], TILE):
             part = dot(attended, w_ref[:, at : at + TILE]).astype(jnp.bfloat16)
             for j, i in enumerate(todo):
-                outs[i][:, at : at + TILE] = part[here[j]]
+                out, to = outs[i], at
+                if isinstance(out, tuple):
+                    out, to = (out[0], at) if at < column else (out[1], at - column)
+                out[:, to : to + TILE] = part[here[j]]
 
     if len(set(outer)) == 1:
         run(outer[0])
@@ -176,23 +185,45 @@
                 out[...] = jnp.zeros_like(out)
 
 
-def add_kernel(*refs, half):
-    *terms, out = refs
-    mine, side, far, direct, early, late = terms
-    for rows, more in ((slice(0, half), [direct, early]), (slice(half, 2 * half), [late])):
-        total = mine[rows].astype(jnp.float32) + side[rows].astype(jnp.float32)
-        total = total + far[rows].astype(jnp.float32)
-        for term in more:
-            total = total + term[...].astype(jnp.float32)
-        out[rows] = total.astype(out.dtype)
-
-
-def call(kernel, out_shape, *args, scratch, limit, place=pltpu.VMEM):
+def project_kernel(att_ref, w_ref, out, *, begin):
+    tp_at = lax.axis_index("tp")
+    is_outer = (tp_at == 0) | (tp_at == 3)
+
+    @pl.when(is_outer)
+    def _():
+        attended = att_ref[...]
+        for at in range(begin, w_ref.shape[1], TILE):
+            part = dot(attended, w_ref[:, at : at + TILE])
+            out[:, at - begin : at - begin + TILE] = part.astype(jnp.bfloat16)
+
+    @pl.when(~is_outer)
+    def _():
+        out[...] = jnp.zeros_like(out)
+
+
+def add_kernel(mine, side, far, direct, early, late, out, sum_ref, sems):
+    column = direct.shape[1]
+    copies = []
+    for i, at in enumerate(range(0, out.shape[0], ROWS)):
+        rows = slice(at, at + ROWS)
+        for cols, more in ((slice(0, column), [direct, early]), (slice(column, None), [late])):
+            total = mine[rows, cols].astype(jnp.float32) + side[rows, cols].astype(jnp.float32)
+            total = total + far[rows, cols].astype(jnp.float32)
+            for term in more:
+                total = total + term[rows].astype(jnp.float32)
+            sum_ref[rows, cols] = total.astype(out.dtype)
+        copies.append(pltpu.make_async_copy(sum_ref.at[rows], out.at[rows], sems.at[i]))
+        copies[-1].start()
+    for copy in copies:
+        copy.wait()
+
+
+def call(kernel, out_shape, *args, scratch, limit, place=pltpu.VMEM, result=pltpu.VMEM):
     return pl.pallas_call(
         kernel,
         out_shape=out_shape,
         in_specs=[pl.BlockSpec(memory_space=place)] * len(args),
-        out_specs=[pl.BlockSpec(memory_space=pltpu.VMEM)] * len(out_shape),
+        out_specs=[pl.BlockSpec(memory_space=result)] * len(out_shape),
         scratch_shapes=scratch,
         compiler_params=pltpu.CompilerParams(vmem_limit_bytes=limit * 2**20),
     )(*args)
@@ -246,13 +277,20 @@
         limit=24,
         place=pl.ANY,
     )
-    blocks[1:] = lax.optimization_barrier((*blocks[1:], q_here, w_here))[: chips - 1]
+    blocks[1:] = [after(block, q_here, w_here) for block in blocks[1:]]
     swapped = [lax.ppermute(block, "seq", swap) for block in blocks]
+    slow = chips // 2
+    swapped[slow] = lax.ppermute(after(blocks[slow], *swapped[1:slow], *swapped[slow + 1 :]), "seq", swap)
     hops = list(range(1, chips))
 
-    def layer(order, rows, seen, state=None, first=True, last=True, outer=(0, 0)):
+    def layer(order, rows, seen, state=None, first=True, last=True, outer=(0, 0), split=None, upto=None):
         chunks = len(order)
         running = [(chunks, kv_here, per_kv * rows, 2 * hd), (chunks, kv_here, per_kv * rows, hd)]
+        widths = [width] * chunks
+        if split:
+            widths[split[0] : split[0] + 1] = [split[1], width - split[1]]
+        if upto:
+            widths = [upto]
         own_blocks = [own, swapped[0]] if first else []
         args = [*own_blocks, *[block for _, block in seen], *(state or []), *([w_here] * last)]
         return call(
@@ -266,8 +304,11 @@
                 hops=[d for d, _ in seen],
                 first=first,
                 last=last,
+                split=split,
+                upto=upto,
             ),
-            [jax.ShapeDtypeStruct((rows, width), jnp.bfloat16)] * chunks
+            [jax.ShapeDtypeStruct((rows, columns), jnp.bfloat16) for columns in widths]
+            + ([jax.ShapeDtypeStruct((rows * chunks, heads * hd), jnp.bfloat16)] if upto else [])
             if last
             else [jax.ShapeDtypeStruct(shape, jnp.float32) for shape in running],
             q_here,
@@ -287,29 +328,41 @@
 
     rows = tok // 4
     far_rows = [lambda at: jnp.where(at < 2, 3, 0)]
-    state = layer(far_rows, rows, got, last=False, outer=(0, 1))
-    (far,) = layer(far_rows, rows, theirs, state, first=False, outer=(0, 1))
+    soon = [(d, block) for d, block in theirs if d != slow]
+    then = [(d, block) for d, block in theirs if d == slow]
+    state = layer(far_rows, rows, got + soon, last=False, outer=(0, 1))
+    begin = width * 3 // 5 // TILE * TILE
+    far, attended = layer(far_rows, rows, then, state, first=False, outer=(0, 1), upto=begin)
     inward, sides = [(0, 1), (3, 2)], [(0, 1), (1, 0), (2, 3), (3, 2)]
-    got_far = lax.ppermute(far, "tp", inward)
-    far_here, near, side, mine = layer(
+    got_far = [lax.ppermute(far, "tp", inward)]
+    (far_rest,) = call(
+        functools.partial(project_kernel, begin=begin),
+        [jax.ShapeDtypeStruct((rows, width - begin), jnp.bfloat16)],
+        attended,
+        w_here,
+        scratch=[],
+        limit=24,
+    )
+    got_far.append(lax.ppermute(far_rest, "tp", inward))
+    column = width * 2 // 5 // TILE * TILE
+    far_here, early, late, side, mine = layer(
         far_rows + [lambda at: jnp.where(at < 2, 2, 1), lambda at: at ^ 1, lambda at: at],
         rows,
         got + theirs,
         outer=(1, 0),
-    )
-    half = rows // 2
-    early, late = near[:half], near[half:]
+        split=(1, column),
+    )
     outward = [(1, 2), (2, 1)]
     got_direct = lax.ppermute(early, "tp", [(0, 2), (3, 1)])
     got_late = lax.ppermute(late, "tp", inward)
     got_side = lax.ppermute(side, "tp", sides)
     got_early = lax.ppermute(early, "tp", outward)
-    total_far = added(got_far, far_here)
+    total_far = added(jnp.concatenate(got_far, axis=1), far_here)
     across_far = lax.ppermute(total_far, "tp", [(1, 3), (2, 0)])
     got_late = after(got_late, got_direct, got_early, total_far)
     across_late = lax.ppermute(added(got_late, late), "tp", outward)
     (out,) = call(
-        functools.partial(add_kernel, half=half),
+        add_kernel,
         [jax.ShapeDtypeStruct(mine.shape, mine.dtype)],
         mine,
         got_side,
@@ -317,8 +370,12 @@
         got_direct,
         got_early,
         across_late,
-        scratch=[],
+        scratch=[
+            pltpu.VMEM(mine.shape, mine.dtype),
+            semaphores((rows // ROWS,)),
+        ],
         limit=24,
+        result=pl.ANY,
     )
     return out
 

time: 73 us -> 72.6 us (level)
  starting transfers between devices: 17.7 us -> 16.6 us
    ppermute x1, waiting for transfers between devices: 12.6 us -> 6.78 us  [body(): got_late = lax.ppermute(late, 'tp', inward)]
    ppermute x1, waiting for transfers between devices: 0.01 us -> 4.41 us  [body(): got_early = lax.ppermute(early, 'tp', outward)]
    ppermute x1, starting transfers between devices: 3.76 us -> 0.01 us  [body(): got_side = lax.ppermute(side, 'tp', sides)]
    ppermute x1 -> x3, waiting for transfers between devices: 2.28 us -> 5.88 us  [the longest x1 4.39 us: body(): got_far.append(lax.ppermute(far_rest, 'tp', inward))]
    ppermute x4 -> x3, waiting for transfers between devices: 1.74 us -> 0.01 us  [body(): swapped = [lax.ppermute(block, 'seq', swap) for block in blocks]]
    ppermute x1, starting transfers between devices: 1.33 us -> 2.72 us  [body(): across_far = lax.ppermute(total_far, 'tp', [(1, 3), (2, 0)])]
    ppermute x1 -> x3, starting transfers between devices: 1.29 us -> 2.6 us  [the longest x1 1.29 us: body(): got_far = [lax.ppermute(far, 'tp', inward)]]
    pallas_call x6 -> x7, Pallas kernels: 12.9 us -> 12.8 us  [call(): pl.pallas_call(kernel, out_shape=out_shape, in_specs=[pl.BlockSpec(memory...]
  transfers between devices with their start and end apart: 14 -> 15, of which waited for: 9 -> 8; matrix products, arithmetic and copies ran while one was open for 0% -> 0% of each run, Pallas kernels for 14% -> 14%
where the time goes in v5:
time: 72.6 us; the launch traced here: 71.4 us
  waiting for transfers between devices  37.5 us (52%)
  starting transfers between devices  16.6 us (23%)
  Pallas kernels  12.8 us (18%)
  local copies, waits for them, and re-layouts  3.98 us (5%)
    pallas_call x7, Pallas kernels, call(): pl.pallas_call(kernel, out_shape=out_shape, in_specs=[pl.BlockSpec(memory...  12.8 us
    ppermute x1, waiting for transfers between devices, body(): got_side = lax.ppermute(side, 'tp', sides)  12.1 us
    ppermute x3, waiting for transfers between devices, body(): blocks.append(lax.ppermute(own, 'seq', pairs))  7.49 us
    ppermute x1, waiting for transfers between devices, body(): got_late = lax.ppermute(late, 'tp', inward)  6.78 us
    ppermute x1, waiting for transfers between devices, body(): got_early = lax.ppermute(early, 'tp', outward)  4.41 us
    ppermute x1, waiting for transfers between devices, body(): got_far.append(lax.ppermute(far_rest, 'tp', inward))  4.39 us
    unnamed x6, local copies, waits for them, and re-layouts  3.98 us
    ppermute x3, starting transfers between devices, body(): blocks.append(lax.ppermute(own, 'seq', pairs))  3.88 us
  transfers between devices with their start and end apart: 15, of which 8 were waited for; matrix products, arithmetic and copies ran while one was open for 0% of the time, Pallas kernels for 14%

profile of v5, /device:TPU:22, one launch (start us, length us, event | category | flops | bytes accessed | tf_op | source)
XLA Modules:
  0.0 71.4 jit_solution(16776287139372104755)
XLA Ops:
  0.0 1.7 %shard_map.47.refs_0_ = bf16[256,512]{1,0:T(8,128)(2,1)} custom-call(bf16[256,1024]{1,0:T(8,128)(2,1)} %keys.1, bf16[256,1024]{1,0:T(8,128)(2,1)} %values.1), custom_call_target="tpu_custom_call" | custom-call | tf_op jit(solution)/shard_map/pallas_call | solution.py:222
  1.8 1.3 %collective-permute-start.3 = (bf16[256,512]{1,0:T(8,128)(2,1)}, bf16[256,512]{1,0:T(8,128)(2,1)S(1)}, u32[]{:S(2)}, u32[]{:S(2)}) collective-permute-start(bf16[256,512]{1,0:T(8,128)(2,1)} %shard_map.47.refs_0_), channel_id=1, source_target_pairs={{0,24},{4,28},{8,16},{12,20},{1,25},{5,29},{9,17},{13,21},{2,26},{... | collective-permute-start | bytes 786440 | tf_op jit(solution)/shard_map/ppermute | solution.py:270
  3.1 1.3 %collective-permute-start.1 = (bf16[256,512]{1,0:T(8,128)(2,1)}, bf16[256,512]{1,0:T(8,128)(2,1)S(1)}, u32[]{:S(2)}, u32[]{:S(2)}) collective-permute-start(bf16[256,512]{1,0:T(8,128)(2,1)} %shard_map.47.refs_0_), channel_id=1, source_target_pairs={{0,8},{4,12},{16,24},{20,28},{1,9},{5,13},{17,25},{21,29},{2,10},{... | collective-permute-start | bytes 786440 | tf_op jit(solution)/shard_map/ppermute | solution.py:270
  4.4 1.3 %collective-permute-start.2 = (bf16[256,512]{1,0:T(8,128)(2,1)}, bf16[256,512]{1,0:T(8,128)(2,1)S(1)}, u32[]{:S(2)}, u32[]{:S(2)}) collective-permute-start(bf16[256,512]{1,0:T(8,128)(2,1)} %shard_map.47.refs_0_), channel_id=1, source_target_pairs={{0,16},{4,20},{8,24},{12,28},{1,17},{5,21},{9,25},{13,29},{2,18},{... | collective-permute-start | bytes 786440 | tf_op jit(solution)/shard_map/ppermute | solution.py:270
  5.7 0.0 copy-start
  5.7 4.0 %copy-done = bf16[1024,5120]{1,0:T(8,128)(2,1)S(1)} copy-done((bf16[1024,5120]{1,0:T(8,128)(2,1)S(1)}, bf16[1024,5120]{1,0:T(8,128)(2,1)}, u32[]{:S(2)}) %copy-start) | copy-done | bytes 10485784
  9.7 0.8 %shard_map.46 = (bf16[256,1024]{1,0:T(8,128)(2,1)S(1)}, bf16[1024,5120]{1,0:T(8,128)(2,1)S(1)}) custom-call(bf16[256,1024]{1,0:T(8,128)(2,1)S(1)} %copy-done.2, bf16[1024,5120]{1,0:T(8,128)(2,1)S(1)} %copy-done), custom_call_target="tpu_custom_call" | custom-call | tf_op jit(solution)/shard_map/pallas_call | solution.py:222
  10.4 3.6 %collective-permute-done.3.refs_4_ = bf16[256,512]{1,0:T(8,128)(2,1)S(1)} collective-permute-done((bf16[256,512]{1,0:T(8,128)(2,1)}, bf16[256,512]{1,0:T(8,128)(2,1)S(1)}, u32[]{:S(2)}, u32[]{:S(2)}) %collective-permute-start.3) | collective-permute-done | bytes 262176 | tf_op jit(solution)/shard_map/ppermute | solution.py:270
  14.0 0.0 collective-permute-done.1.refs_2_
  14.0 0.0 collective-permute-start.4
  14.0 0.5 collective-permute-start.5
  14.5 0.0 collective-permute-start
  14.5 3.9 %collective-permute-done.2.refs_3_ = bf16[256,512]{1,0:T(8,128)(2,1)S(1)} collective-permute-done((bf16[256,512]{1,0:T(8,128)(2,1)}, bf16[256,512]{1,0:T(8,128)(2,1)S(1)}, u32[]{:S(2)}, u32[]{:S(2)}) %collective-permute-start.2) | collective-permute-done | bytes 262176 | tf_op jit(solution)/shard_map/ppermute | solution.py:270
  18.4 0.0 collective-permute-start.6
  18.4 0.0 collective-permute-done.refs_1_
  18.5 1.5 %collective-permute-done.6.refs_6_.refs_0_ = bf16[256,512]{1,0:T(8,128)(2,1)S(1)} collective-permute-done((bf16[256,512]{1,0:T(8,128)(2,1)S(1)}, bf16[256,512]{1,0:T(8,128)(2,1)S(1)}, u32[]{:S(2)}, u32[]{:S(2)}) %collective-permute-start.6) | collective-permute-done | bytes 262176 | tf_op jit(solution)/shard_map/ppermute | solution.py:283
  20.0 1.3 %collective-permute-start.8 = (bf16[64,3072]{1,0:T(8,128)(2,1)S(1)}, bf16[64,3072]{1,0:T(8,128)(2,1)S(1)}, u32[]{:S(2)}, u32[]{:S(2)}) collective-permute-start(bf16[64,3072]{1,0:T(8,128)(2,1)S(1)} %get-tuple-element.31), channel_id=1, source_target_pairs={{0,1},{3,2},{4,5},{7,6},{8,9},{11,10},{12,13},{15,14},{16,17},{19,... | collective-permute-start | bytes 1179656 | tf_op jit(solution)/shard_map/ppermute | solution.py:337
  21.3 1.3 %collective-permute-start.9 = (bf16[64,2048]{1,0:T(8,128)(2,1)S(1)}, bf16[64,2048]{1,0:T(8,128)(2,1)S(1)}, u32[]{:S(2)}, u32[]{:S(2)}) collective-permute-start(bf16[64,2048]{1,0:T(8,128)(2,1)S(1)} %shard_map.51), channel_id=1, source_target_pairs={{0,1},{3,2},{4,5},{7,6},{8,9},{11,10},{12,13},{15,14},{16,17},{19,... | collective-permute-start | bytes 786440 | tf_op jit(solution)/shard_map/ppermute | solution.py:346
  22.6 9.2 %shard_map.48 = (bf16[64,5120]{1,0:T(8,128)(2,1)S(1)}, bf16[64,2048]{1,0:T(8,128)(2,1)S(1)}, bf16[64,3072]{1,0:T(8,128)(2,1)S(1)}, bf16[64,5120]{1,0:T(8,128)(2,1)S(1)}, bf16[64,5120]{1,0:T(8,128)(2,1)S(1)}) custom-call(bf16[256,1024]{1,0:T(8,128)(2,1)S(1)} %get-tuple-element.21.q_ref, bf16[256,512]{1,0:T(8,128)(2,1)S(1)} %copy-done.1, ...), custom_call_target="tpu_custom_call" | custom-call | tf_op jit(solution)/shard_map/pallas_call | solution.py:222
  31.8 2.4 %collective-permute-start.12 = (bf16[64,2048]{1,0:T(8,128)(2,1)S(1)}, bf16[64,2048]{1,0:T(8,128)(2,1)S(1)}, u32[]{:S(2)}, u32[]{:S(2)}) collective-permute-start(bf16[64,2048]{1,0:T(8,128)(2,1)S(1)} %get-tuple-element.34), channel_id=1, source_target_pairs={{1,2},{2,1},{5,6},{6,5},{9,10},{10,9},{13,14},{14,13},{17,18},{18,... | collective-permute-start | bytes 786440 | tf_op jit(solution)/shard_map/ppermute | solution.py:359
  34.2 1.3 %collective-permute-start.11 = (bf16[64,2048]{1,0:T(8,128)(2,1)S(1)}, bf16[64,2048]{1,0:T(8,128)(2,1)S(1)}, u32[]{:S(2)}, u32[]{:S(2)}) collective-permute-start(bf16[64,2048]{1,0:T(8,128)(2,1)S(1)} %get-tuple-element.34), channel_id=1, source_target_pairs={{0,2},{3,1},{4,6},{7,5},{8,10},{11,9},{12,14},{15,13},{16,18},{19,... | collective-permute-start | bytes 786440 | tf_op jit(solution)/shard_map/ppermute | solution.py:356
  35.5 1.3 %collective-permute-start.13 = (bf16[64,3072]{1,0:T(8,128)(2,1)S(1)}, bf16[64,3072]{1,0:T(8,128)(2,1)S(1)}, u32[]{:S(2)}, u32[]{:S(2)}) collective-permute-start(bf16[64,3072]{1,0:T(8,128)(2,1)S(1)} %get-tuple-element.35), channel_id=1, source_target_pairs={{0,1},{3,2},{4,5},{7,6},{8,9},{11,10},{12,13},{15,14},{16,17},{19,... | collective-permute-start | bytes 1179656 | tf_op jit(solution)/shard_map/ppermute | solution.py:357
  36.8 4.4 %collective-permute-done.9 = bf16[64,2048]{1,0:T(8,128)(2,1)S(1)} collective-permute-done((bf16[64,2048]{1,0:T(8,128)(2,1)S(1)}, bf16[64,2048]{1,0:T(8,128)(2,1)S(1)}, u32[]{:S(2)}, u32[]{:S(2)}) %collective-permute-start.9) | collective-permute-done | bytes 262176 | tf_op jit(solution)/shard_map/ppermute | solution.py:346
  41.2 0.2 add_convert_fusion
  41.3 2.7 %collective-permute-start.10 = (bf16[64,5120]{1,0:T(8,128)(2,1)S(1)}, bf16[64,5120]{1,0:T(8,128)(2,1)S(1)}, u32[]{:S(2)}, u32[]{:S(2)}) collective-permute-start(bf16[64,5120]{1,0:T(8,128)(2,1)S(1)} %add_convert_fusion), channel_id=1, source_target_pairs={{1,3},{2,0},{5,7},{6,4},{9,11},{10,8},{13,15},{14,12},{17,19},{18,... | collective-permute-start | bytes 1966088 | tf_op jit(solution)/shard_map/ppermute | solution.py:361
  44.1 4.4 %collective-permute-done.12.early = bf16[64,2048]{1,0:T(8,128)(2,1)S(1)} collective-permute-done((bf16[64,2048]{1,0:T(8,128)(2,1)S(1)}, bf16[64,2048]{1,0:T(8,128)(2,1)S(1)}, u32[]{:S(2)}, u32[]{:S(2)}) %collective-permute-start.12) | collective-permute-done | bytes 262176 | tf_op jit(solution)/shard_map/ppermute | solution.py:359
  48.5 6.8 %collective-permute-done.13 = bf16[64,3072]{1,0:T(8,128)(2,1)S(1)} collective-permute-done((bf16[64,3072]{1,0:T(8,128)(2,1)S(1)}, bf16[64,3072]{1,0:T(8,128)(2,1)S(1)}, u32[]{:S(2)}, u32[]{:S(2)}) %collective-permute-start.13) | collective-permute-done | bytes 393248 | tf_op jit(solution)/shard_map/ppermute | solution.py:357
  55.3 0.1 add_convert_fusion.1
  55.4 1.9 %collective-permute-start.14 = (bf16[64,3072]{1,0:T(8,128)(2,1)S(1)}, bf16[64,3072]{1,0:T(8,128)(2,1)S(1)}, u32[]{:S(2)}, u32[]{:S(2)}) collective-permute-start(bf16[64,3072]{1,0:T(8,128)(2,1)S(1)} %add_convert_fusion.1), channel_id=1, source_target_pairs={{1,2},{2,1},{5,6},{6,5},{9,10},{10,9},{13,14},{14,13},{17,18},{18,... | collective-permute-start | bytes 1179656 | tf_op jit(solution)/shard_map/ppermute | solution.py:363
  57.3 12.1 %collective-permute-done.7.side = bf16[64,5120]{1,0:T(8,128)(2,1)S(1)} collective-permute-done((bf16[64,5120]{1,0:T(8,128)(2,1)S(1)}, bf16[64,5120]{1,0:T(8,128)(2,1)S(1)}, u32[]{:S(2)}, u32[]{:S(2)}) %collective-permute-start.7) | collective-permute-done | bytes 655392 | tf_op jit(solution)/shard_map/ppermute | solution.py:358
  69.4 0.8 %collective-permute-done.14.late = bf16[64,3072]{1,0:T(8,128)(2,1)S(1)} collective-permute-done((bf16[64,3072]{1,0:T(8,128)(2,1)S(1)}, bf16[64,3072]{1,0:T(8,128)(2,1)S(1)}, u32[]{:S(2)}, u32[]{:S(2)}) %collective-permute-start.14) | collective-permute-done | bytes 393248 | tf_op jit(solution)/shard_map/ppermute | solution.py:363
  70.2 1.1 %shard_map.52 = bf16[64,5120]{1,0:T(8,128)(2,1)} custom-call(bf16[64,5120]{1,0:T(8,128)(2,1)S(1)} %get-tuple-element.27.mine, bf16[64,5120]{1,0:T(8,128)(2,1)S(1)} %collective-permute-done.7.side, bf16[64,5120]{1,0:T(8,128)(2,1)S(1)} %collective-permute-done.10.far, bf16[64,2048]{1,0:T(8,128)(2,1)S(1)} %collective-permute-done.11.direct, ...), custom_call_target="tpu_custom_call" | custom-call | tf_op jit(solution)/shard_map/pallas_call | solution.py:222
  (13 shorter events, 0.1 us)
Async XLA Ops:
  0.0 5.7 %copy-start.2 = (bf16[256,1024]{1,0:T(8,128)(2,1)S(1)}, bf16[256,1024]{1,0:T(8,128)(2,1)}, u32[]{:S(2)}) copy-start(bf16[256,1024]{1,0:T(8,128)(2,1)} %refs_0_.1) | copy-start | bytes 1572868
  1.8 12.2 %collective-permute-start.3 = (bf16[256,512]{1,0:T(8,128)(2,1)}, bf16[256,512]{1,0:T(8,128)(2,1)S(1)}, u32[]{:S(2)}, u32[]{:S(2)}) collective-permute-start(bf16[256,512]{1,0:T(8,128)(2,1)} %shard_map.47.refs_0_), channel_id=1, source_target_pairs={{0,24},{4,28},{8,16},{12,20},{1,25},{5,29},{9,17},{13,21},{2,26},{... | collective-permute-start | bytes 786440 | tf_op jit(solution)/shard_map/ppermute | solution.py:270
  3.1 10.9 %collective-permute-start.1 = (bf16[256,512]{1,0:T(8,128)(2,1)}, bf16[256,512]{1,0:T(8,128)(2,1)S(1)}, u32[]{:S(2)}, u32[]{:S(2)}) collective-permute-start(bf16[256,512]{1,0:T(8,128)(2,1)} %shard_map.47.refs_0_), channel_id=1, source_target_pairs={{0,8},{4,12},{16,24},{20,28},{1,9},{5,13},{17,25},{21,29},{2,10},{... | collective-permute-start | bytes 786440 | tf_op jit(solution)/shard_map/ppermute | solution.py:270
  4.4 14.1 %collective-permute-start.2 = (bf16[256,512]{1,0:T(8,128)(2,1)}, bf16[256,512]{1,0:T(8,128)(2,1)S(1)}, u32[]{:S(2)}, u32[]{:S(2)}) collective-permute-start(bf16[256,512]{1,0:T(8,128)(2,1)} %shard_map.47.refs_0_), channel_id=1, source_target_pairs={{0,16},{4,20},{8,24},{12,28},{1,17},{5,21},{9,25},{13,29},{2,18},{... | collective-permute-start | bytes 786440 | tf_op jit(solution)/shard_map/ppermute | solution.py:270
  5.7 4.0 %copy-start = (bf16[1024,5120]{1,0:T(8,128)(2,1)S(1)}, bf16[1024,5120]{1,0:T(8,128)(2,1)}, u32[]{:S(2)}) copy-start(bf16[1024,5120]{1,0:T(8,128)(2,1)} %refs_1_.1) | copy-start | bytes 31457284
  9.6 4.9 %copy-start.1 = (bf16[256,512]{1,0:T(8,128)(2,1)S(1)}, bf16[256,512]{1,0:T(8,128)(2,1)}, u32[]{:S(2)}) copy-start(bf16[256,512]{1,0:T(8,128)(2,1)} %shard_map.47.refs_0_) | copy-start | bytes 786436
  14.0 4.4 %collective-permute-start.4 = (bf16[256,512]{1,0:T(8,128)(2,1)S(1)}, bf16[256,512]{1,0:T(8,128)(2,1)S(1)}, u32[]{:S(2)}, u32[]{:S(2)}) collective-permute-start(bf16[256,512]{1,0:T(8,128)(2,1)S(1)} %collective-permute-done.1.refs_2_), channel_id=1, source_target_pairs={{0,4},{4,0},{8,12},{12,8},{16,20},{20,16},{24,28},{28,24},{1,5},{5... | collective-permute-start | bytes 786440 | tf_op jit(solution)/shard_map/ppermute | solution.py:281
  14.0 4.4 %collective-permute-start.5 = (bf16[256,512]{1,0:T(8,128)(2,1)S(1)}, bf16[256,512]{1,0:T(8,128)(2,1)S(1)}, u32[]{:S(2)}, u32[]{:S(2)}) collective-permute-start(bf16[256,512]{1,0:T(8,128)(2,1)S(1)} %collective-permute-done.3.refs_4_), channel_id=1, source_target_pairs={{0,4},{4,0},{8,12},{12,8},{16,20},{20,16},{24,28},{28,24},{1,5},{5... | collective-permute-start | bytes 786440 | tf_op jit(solution)/shard_map/ppermute | solution.py:281
  14.5 3.9 %collective-permute-start = (bf16[256,512]{1,0:T(8,128)(2,1)S(1)}, bf16[256,512]{1,0:T(8,128)(2,1)S(1)}, u32[]{:S(2)}, u32[]{:S(2)}) collective-permute-start(bf16[256,512]{1,0:T(8,128)(2,1)S(1)} %copy-done.1), channel_id=1, source_target_pairs={{0,4},{4,0},{8,12},{12,8},{16,20},{20,16},{24,28},{28,24},{1,5},{5... | collective-permute-start | bytes 786440 | tf_op jit(solution)/shard_map/ppermute | solution.py:281
  18.4 1.5 %collective-permute-start.6 = (bf16[256,512]{1,0:T(8,128)(2,1)S(1)}, bf16[256,512]{1,0:T(8,128)(2,1)S(1)}, u32[]{:S(2)}, u32[]{:S(2)}) collective-permute-start(bf16[256,512]{1,0:T(8,128)(2,1)S(1)} %collective-permute-done.2.refs_3_), channel_id=1, source_target_pairs={{0,4},{4,0},{8,12},{12,8},{16,20},{20,16},{24,28},{28,24},{1,5},{5... | collective-permute-start | bytes 786440 | tf_op jit(solution)/shard_map/ppermute | solution.py:283
  20.0 21.2 %collective-permute-start.8 = (bf16[64,3072]{1,0:T(8,128)(2,1)S(1)}, bf16[64,3072]{1,0:T(8,128)(2,1)S(1)}, u32[]{:S(2)}, u32[]{:S(2)}) collective-permute-start(bf16[64,3072]{1,0:T(8,128)(2,1)S(1)} %get-tuple-element.31), channel_id=1, source_target_pairs={{0,1},{3,2},{4,5},{7,6},{8,9},{11,10},{12,13},{15,14},{16,17},{19,... | collective-permute-start | bytes 1179656 | tf_op jit(solution)/shard_map/ppermute | solution.py:337
  21.3 19.8 %collective-permute-start.9 = (bf16[64,2048]{1,0:T(8,128)(2,1)S(1)}, bf16[64,2048]{1,0:T(8,128)(2,1)S(1)}, u32[]{:S(2)}, u32[]{:S(2)}) collective-permute-start(bf16[64,2048]{1,0:T(8,128)(2,1)S(1)} %shard_map.51), channel_id=1, source_target_pairs={{0,1},{3,2},{4,5},{7,6},{8,9},{11,10},{12,13},{15,14},{16,17},{19,... | collective-permute-start | bytes 786440 | tf_op jit(solution)/shard_map/ppermute | solution.py:346
  31.8 16.7 %collective-permute-start.12 = (bf16[64,2048]{1,0:T(8,128)(2,1)S(1)}, bf16[64,2048]{1,0:T(8,128)(2,1)S(1)}, u32[]{:S(2)}, u32[]{:S(2)}) collective-permute-start(bf16[64,2048]{1,0:T(8,128)(2,1)S(1)} %get-tuple-element.34), channel_id=1, source_target_pairs={{1,2},{2,1},{5,6},{6,5},{9,10},{10,9},{13,14},{14,13},{17,18},{18,... | collective-permute-start | bytes 786440 | tf_op jit(solution)/shard_map/ppermute | solution.py:359
  34.2 14.3 %collective-permute-start.11 = (bf16[64,2048]{1,0:T(8,128)(2,1)S(1)}, bf16[64,2048]{1,0:T(8,128)(2,1)S(1)}, u32[]{:S(2)}, u32[]{:S(2)}) collective-permute-start(bf16[64,2048]{1,0:T(8,128)(2,1)S(1)} %get-tuple-element.34), channel_id=1, source_target_pairs={{0,2},{3,1},{4,6},{7,5},{8,10},{11,9},{12,14},{15,13},{16,18},{19,... | collective-permute-start | bytes 786440 | tf_op jit(solution)/shard_map/ppermute | solution.py:356
  35.5 19.8 %collective-permute-start.13 = (bf16[64,3072]{1,0:T(8,128)(2,1)S(1)}, bf16[64,3072]{1,0:T(8,128)(2,1)S(1)}, u32[]{:S(2)}, u32[]{:S(2)}) collective-permute-start(bf16[64,3072]{1,0:T(8,128)(2,1)S(1)} %get-tuple-element.35), channel_id=1, source_target_pairs={{0,1},{3,2},{4,5},{7,6},{8,9},{11,10},{12,13},{15,14},{16,17},{19,... | collective-permute-start | bytes 1179656 | tf_op jit(solution)/shard_map/ppermute | solution.py:357
  41.2 28.2 %collective-permute-start.7 = (bf16[64,5120]{1,0:T(8,128)(2,1)S(1)}, bf16[64,5120]{1,0:T(8,128)(2,1)S(1)}, u32[]{:S(2)}, u32[]{:S(2)}) collective-permute-start(bf16[64,5120]{1,0:T(8,128)(2,1)S(1)} %get-tuple-element.28), channel_id=1, source_target_pairs={{0,1},{1,0},{2,3},{3,2},{4,5},{5,4},{6,7},{7,6},{8,9},{9,8},{10,11... | collective-permute-start | bytes 1966088 | tf_op jit(solution)/shard_map/ppermute | solution.py:358
  41.3 28.9 %collective-permute-start.10 = (bf16[64,5120]{1,0:T(8,128)(2,1)S(1)}, bf16[64,5120]{1,0:T(8,128)(2,1)S(1)}, u32[]{:S(2)}, u32[]{:S(2)}) collective-permute-start(bf16[64,5120]{1,0:T(8,128)(2,1)S(1)} %add_convert_fusion), channel_id=1, source_target_pairs={{1,3},{2,0},{5,7},{6,4},{9,11},{10,8},{13,15},{14,12},{17,19},{18,... | collective-permute-start | bytes 1966088 | tf_op jit(solution)/shard_map/ppermute | solution.py:361
  55.4 14.8 %collective-permute-start.14 = (bf16[64,3072]{1,0:T(8,128)(2,1)S(1)}, bf16[64,3072]{1,0:T(8,128)(2,1)S(1)}, u32[]{:S(2)}, u32[]{:S(2)}) collective-permute-start(bf16[64,3072]{1,0:T(8,128)(2,1)S(1)} %add_convert_fusion.1), channel_id=1, source_target_pairs={{1,2},{2,1},{5,6},{6,5},{9,10},{10,9},{13,14},{14,13},{17,18},{18,... | collective-permute-start | bytes 1179656 | tf_op jit(solution)/shard_map/ppermute | solution.py:363
